TPU v7x, 32 devices: a whole 2x2x4 slice. The times are simulated.
32 devices in a mesh: row: 8 (over y, x, core), col: 4 (over z).
Axes of the slice: x: 2, y: 2, z: 4, core: 2. Of those that a mesh axis runs over, the one named last changes fastest.
Arguments:
- a_panels: bfloat16 [8, 4, 16, 256, 256], P('row', 'col'), may hold values from -1.5 to 1.5
- b_panels: bfloat16 [8, 4, 16, 256, 256], P('row', 'col'), may hold values from -1.5 to 1.5
- a_rows: int32 [8, 4, 16], replicated, may hold values from 0 to 23, as said below
- a_inner: int32 [8, 4, 16], replicated, may hold values from 0 to 23, as said below
- b_inner: int32 [8, 4, 16], replicated, may hold values from 0 to 23, as said below
- b_cols: int32 [8, 4, 16], replicated, may hold values from 0 to 23, as said below
- c_rows: int32 [8, 4, 64], replicated, may hold values from 0 to 23, as said below
- c_cols: int32 [8, 4, 64], replicated, may hold values from 0 to 23
Outputs:
- c_blocks: bfloat16 [8, 4, 64, 256, 256], P('row', 'col')
Inputs may be any that keep to these rules, and one draw needn't show every extreme that they name: `a_rows`: the blocks of one left panel stand at distinct positions; the left blocks and result blocks of one grid row use the same 8 block rows. `a_inner`: all left and right panels draw their inner indices from one common set of 8 indices, which holds 23; every left panel uses 24 - 1. `b_inner`: every right panel holds each index of the common set exactly twice. `b_cols`: the blocks of one right panel stand at distinct positions; the right blocks and result blocks of one grid column use the same 8 block columns. `c_rows`: the 64 result positions of one grid position are distinct and cover every pair of its grid row's block rows and its grid column's block columns.
All inputs are finite; a program needn't handle non-finite values.
Results may differ from a plain program's by a relative error of at most 0.001.
Values may be sent and summed in bfloat16 or wider, within the bound.
No kernel may reach another device: no remote copies, remote signals or barrier semaphores. Data moves between devices by JAX's collectives and lax.ppermute only.
A program may use at most 128 MiB of HBM per device.

v0:
```python
import jax
import jax.numpy as jnp
from jax import lax
from jax.sharding import PartitionSpec as P

STEPS = 4


def shifted(value, axis, steps):
    count = lax.axis_size(axis)
    pairs = [(source, (source + steps) % count) for source in range(count)]
    return lax.ppermute(value, axis, pairs)


def pick_pairs(left_inner, right_inner):
    count = right_inner.shape[0]
    places = jnp.arange(count, dtype=jnp.int32)
    matches = left_inner[:, None] == right_inner[None, :]
    first_pick = jnp.min(jnp.where(matches, places[None, :], count), axis=1)
    later = matches & (places[None, :] > first_pick[:, None])
    second_pick = jnp.min(jnp.where(later, places[None, :], count), axis=1)
    right_pick = jnp.stack([first_pick, second_pick], axis=1).reshape(-1)
    left_pick = jnp.repeat(jnp.arange(left_inner.shape[0], dtype=jnp.int32), 2)
    usable = right_pick < count
    return (left_pick, jnp.minimum(right_pick, count - 1), usable)


def target_slots(left_rows, right_cols, own_rows, own_cols, usable):
    slot_count = own_rows.shape[0]
    hit_table = (left_rows[:, None] == own_rows[None, :]) & (
        right_cols[:, None] == own_cols[None, :]
    )
    places = jnp.arange(slot_count, dtype=jnp.int32)
    found_slot = jnp.min(jnp.where(hit_table, places[None, :], slot_count), axis=1)
    return jnp.where(usable, found_slot, slot_count)


def accumulate(
    totals,
    left_blocks,
    right_blocks,
    left_rows,
    left_inner,
    right_inner,
    right_cols,
    own_rows,
    own_cols,
):
    left_pick, right_pick, usable = pick_pairs(left_inner, right_inner)
    slots = target_slots(left_rows[left_pick], right_cols[right_pick], own_rows, own_cols, usable)
    products = jnp.einsum(
        "pik,pkj->pij",
        left_blocks[left_pick],
        right_blocks[right_pick],
        preferred_element_type=jnp.float32,
    )
    return totals.at[slots].add(products, mode="drop")


def on_device(a_panels, b_panels, a_rows, a_inner, b_inner, b_cols, c_rows, c_cols):
    row_id = lax.axis_index("row")
    col_id = lax.axis_index("col")
    row_count = lax.axis_size("row")
    col_count = lax.axis_size("col")
    left_start = a_panels[0, 0]
    right_start = b_panels[0, 0]
    left_now = left_start
    right_now = right_start
    own_rows = c_rows[row_id, col_id]
    own_cols = c_cols[row_id, col_id]
    block_width = a_panels.shape[3]
    totals = jnp.zeros((c_rows.shape[2], block_width, block_width), jnp.float32)
    for shift_step in range(STEPS):
        if shift_step > 0:
            left_now = shifted(left_now, "col", -1)
            right_now = shifted(right_now, "row", -1)
        left_col = (col_id + shift_step) % col_count
        right_row = (row_id + shift_step) % row_count
        totals = accumulate(
            totals,
            left_now,
            right_now,
            a_rows[row_id, left_col],
            a_inner[row_id, left_col],
            b_inner[right_row, col_id],
            b_cols[right_row, col_id],
            own_rows,
            own_cols,
        )
    return totals.astype(jnp.bfloat16)[None, None]


def solution(mesh):
    in_specs = (
        P("row", "col", None, None, None),
        P("row", "col", None, None, None),
        P(),
        P(),
        P(),
        P(),
        P(),
        P(),
    )
    out_specs = P("row", "col", None, None, None)
    return jax.shard_map(
        on_device, mesh=mesh, in_specs=in_specs, out_specs=out_specs, check_vma=False
    )
```

profile of v0, /device:TPU:0, one launch (start us, length us, event | category | flops | bytes accessed | tf_op | source)
XLA Modules:
  0.0 243.6 jit_solution(5964939774667920126)
XLA Ops:
  0.0 3.3 %collective-permute-start.1 = (bf16[16,256,256]{2,1,0:T(8,128)(2,1)}, bf16[16,256,256]{2,1,0:T(8,128)(2,1)}, u32[]{:S(2)}, u32[]{:S(2)}) collective-permute-start(bf16[16,256,256]{2,1,0:T(8,128)(2,1)} %bitcast.90), channel_id=1, source_target_pairs={{0,28},{4,0},{8,4},{12,8},{16,12},{20,16},{24,20},{28,24},{1,29},{... | collective-permute-start | bytes 6291464 | tf_op jit(solution)/shard_map/ppermute | solution.py:12
  3.3 3.6 %collective-permute-start = (bf16[16,256,256]{2,1,0:T(8,128)(2,1)}, bf16[16,256,256]{2,1,0:T(8,128)(2,1)}, u32[]{:S(2)}, u32[]{:S(2)}) collective-permute-start(bf16[16,256,256]{2,1,0:T(8,128)(2,1)} %bitcast.92), channel_id=1, source_target_pairs={{0,3},{1,0},{2,1},{3,2},{4,7},{5,4},{6,5},{7,6},{8,11},{9,8},{10,9... | collective-permute-start | bytes 6291464 | tf_op jit(solution)/shard_map/ppermute | solution.py:12
  6.9 0.7 fusion.24
  7.7 0.8 fusion.23
  8.5 0.2 fusion.1
  8.9 0.2 select_reduce_fusion.6
  9.1 0.2 select_reduce_fusion.7
  9.5 4.5 %gather_fusion.3 = bf16[32,256,256]{2,1,0:T(8,128)(2,1)} fusion(bf16[16,256,256]{2,1,0:T(8,128)(2,1)} %bitcast.91, s32[1024]{0:T(1024)S(1)} %pad_clamp_fusion.3), kind=kCustom, calls=%fused_computation.3 | custom fusion | bytes 8388736 | tf_op jit(solution)/shard_map/gather | solution.py:54
  14.1 2.7 %gather_fusion.2 = bf16[32,256,256]{2,1,0:T(8,128)(2,1)} fusion(bf16[16,256,256]{2,1,0:T(8,128)(2,1)S(1)} %bitcast.93, s32[1024]{0:T(1024)S(1)} %pad_clamp_fusion.4), kind=kCustom, calls=%fused_computation.2 | custom fusion | bytes 8388736 | tf_op jit(solution)/shard_map/gather | solution.py:53
  16.9 0.7 fusion.17
  17.6 0.7 gather_fusion.1
  18.3 0.2 fusion.2
  18.5 0.2 fusion.3
  18.7 0.2 select_reduce_fusion.5
  18.9 0.2 select_reduce_fusion.4
  19.6 0.8 fusion.15
  20.4 0.7 gather_fusion
  21.1 0.7 gather_fusion.12
  21.8 0.7 gather_fusion.4
  22.6 0.7 gather_fusion.8
  23.3 3.9 %collective-permute-done.1 = bf16[16,256,256]{2,1,0:T(8,128)(2,1)} collective-permute-done((bf16[16,256,256]{2,1,0:T(8,128)(2,1)}, bf16[16,256,256]{2,1,0:T(8,128)(2,1)}, u32[]{:S(2)}, u32[]{:S(2)}) %collective-permute-start.1) | collective-permute-done | bytes 2097184 | tf_op jit(solution)/shard_map/ppermute | solution.py:12
  27.2 2.8 %collective-permute-start.3 = (bf16[16,256,256]{2,1,0:T(8,128)(2,1)}, bf16[16,256,256]{2,1,0:T(8,128)(2,1)S(1)}, u32[]{:S(2)}, u32[]{:S(2)}) collective-permute-start(bf16[16,256,256]{2,1,0:T(8,128)(2,1)} %collective-permute-done.1), channel_id=1, source_target_pairs={{0,28},{4,0},{8,4},{12,8},{16,12},{20,16},{24,20},{28,24},{1,29},{... | collective-permute-start | bytes 6291464 | tf_op jit(solution)/shard_map/ppermute | solution.py:12
  30.0 20.9 %collective-permute-done = bf16[16,256,256]{2,1,0:T(8,128)(2,1)} collective-permute-done((bf16[16,256,256]{2,1,0:T(8,128)(2,1)}, bf16[16,256,256]{2,1,0:T(8,128)(2,1)}, u32[]{:S(2)}, u32[]{:S(2)}) %collective-permute-start) | collective-permute-done | bytes 2097184 | tf_op jit(solution)/shard_map/ppermute | solution.py:12
  50.9 4.3 %collective-permute-start.2 = (bf16[16,256,256]{2,1,0:T(8,128)(2,1)}, bf16[16,256,256]{2,1,0:T(8,128)(2,1)}, u32[]{:S(2)}, u32[]{:S(2)}) collective-permute-start(bf16[16,256,256]{2,1,0:T(8,128)(2,1)} %collective-permute-done), channel_id=1, source_target_pairs={{0,3},{1,0},{2,1},{3,2},{4,7},{5,4},{6,5},{7,6},{8,11},{9,8},{10,9... | collective-permute-start | bytes 6291464 | tf_op jit(solution)/shard_map/ppermute | solution.py:12
  56.1 0.7 gather_fusion.13
  56.8 0.7 gather_fusion.5
  57.5 0.7 gather_fusion.9
  58.2 0.7 fusion.16
  58.9 0.2 select_reduce_fusion
  59.1 8.1 %fusion.31 = f32[32,256,256]{2,1,0:T(8,128)} fusion(bf16[32,256,256]{2,1,0:T(8,128)(2,1)} %gather_fusion.2, bf16[32,256,256]{2,1,0:T(8,128)(2,1)} %gather_fusion.3), kind=kOutput, calls=%fused_computation.120 | convolution fusion | flops 1073741824 | bytes 16777216 | tf_op jit(solution)/shard_map/pik,pkj->pij/dot_general | solution.py:51
  67.3 1.5 collective-permute-start.5
  68.8 29.5 %collective-permute-done.2 = bf16[16,256,256]{2,1,0:T(8,128)(2,1)} collective-permute-done((bf16[16,256,256]{2,1,0:T(8,128)(2,1)}, bf16[16,256,256]{2,1,0:T(8,128)(2,1)}, u32[]{:S(2)}, u32[]{:S(2)}) %collective-permute-start.2) | collective-permute-done | bytes 2097184 | tf_op jit(solution)/shard_map/ppermute | solution.py:12
  98.3 4.3 %collective-permute-start.4 = (bf16[16,256,256]{2,1,0:T(8,128)(2,1)}, bf16[16,256,256]{2,1,0:T(8,128)(2,1)}, u32[]{:S(2)}, u32[]{:S(2)}) collective-permute-start(bf16[16,256,256]{2,1,0:T(8,128)(2,1)} %collective-permute-done.2), channel_id=1, source_target_pairs={{0,3},{1,0},{2,1},{3,2},{4,7},{5,4},{6,5},{7,6},{8,11},{9,8},{10,9... | collective-permute-start | bytes 6291464 | tf_op jit(solution)/shard_map/ppermute | solution.py:12
  102.6 7.8 %broadcast_in_dim.173 = f32[64,256,256]{2,1,0:T(8,128)} broadcast(f32[]{:T(128)} %constant.60.clone.1), dimensions={} | broadcast | bytes 16777220 | tf_op jit(solution)/shard_map/broadcast_in_dim | solution.py:72
  110.3 19.0 %scatter_fusion = f32[64,256,256]{2,1,0:T(8,128)} fusion(f32[64,256,256]{2,1,0:T(8,128)} %broadcast_in_dim.173, s32[32]{0:T(128)S(1)} %fusion.6, f32[32,256,256]{2,1,0:T(8,128)} %fusion.31), kind=kCustom, calls=%fused_computation.16 | custom fusion | flops 2097152 | bytes 25165952 | tf_op jit(solution)/shard_map/scatter-add | solution.py:57
  129.3 4.3 %gather_fusion.7 = bf16[32,256,256]{2,1,0:T(8,128)(2,1)} fusion(bf16[16,256,256]{2,1,0:T(8,128)(2,1)} %collective-permute-done.1, s32[1024]{0:T(1024)S(1)} %pad_clamp_fusion.2), kind=kCustom, calls=%fused_computation.7 | custom fusion | bytes 8388736 | tf_op jit(solution)/shard_map/gather | solution.py:54
  133.7 4.4 %gather_fusion.6 = bf16[32,256,256]{2,1,0:T(8,128)(2,1)} fusion(bf16[16,256,256]{2,1,0:T(8,128)(2,1)} %collective-permute-done, s32[1024]{0:T(1024)S(1)} %pad_clamp_fusion.4), kind=kCustom, calls=%fused_computation.6 | custom fusion | bytes 8388736 | tf_op jit(solution)/shard_map/gather | solution.py:53
  138.0 8.1 %fusion.32 = f32[32,256,256]{2,1,0:T(8,128)} fusion(bf16[32,256,256]{2,1,0:T(8,128)(2,1)} %gather_fusion.6, bf16[32,256,256]{2,1,0:T(8,128)(2,1)} %gather_fusion.7), kind=kOutput, calls=%fused_computation.121 | convolution fusion | flops 1073741824 | bytes 16777216 | tf_op jit(solution)/shard_map/pik,pkj->pij/dot_general | solution.py:51
  146.2 18.7 %scatter_fusion.1 = f32[64,256,256]{2,1,0:T(8,128)} fusion(f32[64,256,256]{2,1,0:T(8,128)} %scatter_fusion, s32[32]{0:T(128)S(1)} %fusion.8, f32[32,256,256]{2,1,0:T(8,128)} %fusion.32), kind=kCustom, calls=%fused_computation.17 | custom fusion | flops 2097152 | bytes 25165952 | tf_op jit(solution)/shard_map/scatter-add | solution.py:57
  164.8 2.8 %gather_fusion.11 = bf16[32,256,256]{2,1,0:T(8,128)(2,1)} fusion(bf16[16,256,256]{2,1,0:T(8,128)(2,1)S(1)} %collective-permute-done.3, s32[1024]{0:T(1024)S(1)} %pad_clamp_fusion.1), kind=kCustom, calls=%fused_computation.11 | custom fusion | bytes 8388736 | tf_op jit(solution)/shard_map/gather | solution.py:54
  167.6 4.3 %gather_fusion.10 = bf16[32,256,256]{2,1,0:T(8,128)(2,1)} fusion(bf16[16,256,256]{2,1,0:T(8,128)(2,1)} %collective-permute-done.2, s32[1024]{0:T(1024)S(1)} %pad_clamp_fusion.4), kind=kCustom, calls=%fused_computation.10 | custom fusion | bytes 8388736 | tf_op jit(solution)/shard_map/gather | solution.py:53
  171.9 8.1 %fusion.33 = f32[32,256,256]{2,1,0:T(8,128)} fusion(bf16[32,256,256]{2,1,0:T(8,128)(2,1)} %gather_fusion.10, bf16[32,256,256]{2,1,0:T(8,128)(2,1)} %gather_fusion.11), kind=kOutput, calls=%fused_computation.122 | convolution fusion | flops 1073741824 | bytes 16777216 | tf_op jit(solution)/shard_map/pik,pkj->pij/dot_general | solution.py:51
  180.1 18.8 %scatter_fusion.2 = f32[64,256,256]{2,1,0:T(8,128)} fusion(f32[64,256,256]{2,1,0:T(8,128)} %scatter_fusion.1, s32[32]{0:T(128)S(1)} %fusion.10, f32[32,256,256]{2,1,0:T(8,128)} %fusion.33), kind=kCustom, calls=%fused_computation.18 | custom fusion | flops 2097152 | bytes 25165952 | tf_op jit(solution)/shard_map/scatter-add | solution.py:57
  198.9 4.3 %gather_fusion.15 = bf16[32,256,256]{2,1,0:T(8,128)(2,1)} fusion(bf16[16,256,256]{2,1,0:T(8,128)(2,1)} %collective-permute-done.5, s32[1024]{0:T(1024)S(1)} %pad_clamp_fusion), kind=kCustom, calls=%fused_computation.15 | custom fusion | bytes 8388736 | tf_op jit(solution)/shard_map/gather | solution.py:54
  203.2 4.4 %gather_fusion.14 = bf16[32,256,256]{2,1,0:T(8,128)(2,1)} fusion(bf16[16,256,256]{2,1,0:T(8,128)(2,1)} %collective-permute-done.4, s32[1024]{0:T(1024)S(1)} %pad_clamp_fusion.4), kind=kCustom, calls=%fused_computation.14 | custom fusion | bytes 8388736 | tf_op jit(solution)/shard_map/gather | solution.py:53
  207.6 8.1 %fusion.34 = f32[32,256,256]{2,1,0:T(8,128)} fusion(bf16[32,256,256]{2,1,0:T(8,128)(2,1)} %gather_fusion.14, bf16[32,256,256]{2,1,0:T(8,128)(2,1)} %gather_fusion.15), kind=kOutput, calls=%fused_computation.123 | convolution fusion | flops 1073741824 | bytes 16777216 | tf_op jit(solution)/shard_map/pik,pkj->pij/dot_general | solution.py:51
  215.7 18.9 %scatter_fusion.3 = f32[64,256,256]{2,1,0:T(8,128)} fusion(f32[64,256,256]{2,1,0:T(8,128)} %scatter_fusion.2, s32[32]{0:T(128)S(1)} %fusion.12, f32[32,256,256]{2,1,0:T(8,128)} %fusion.34), kind=kCustom, calls=%fused_computation.19 | custom fusion | flops 2097152 | bytes 25165952 | tf_op jit(solution)/shard_map/scatter-add | solution.py:57
  234.6 8.9 %convert_bitcast_fusion = bf16[1,1,64,256,256]{4,3,2,1,0:T(8,128)(2,1)} fusion(f32[64,256,256]{2,1,0:T(8,128)} %scatter_fusion.3), kind=kLoop, calls=%fused_computation.20 | loop fusion | flops 4194304 | bytes 25165824 | tf_op jit(solution)/shard_map/broadcast_in_dim | solution.py:90
  (42 shorter events, 1.9 us)
Async XLA Ops:
  0.0 27.2 %collective-permute-start.1 = (bf16[16,256,256]{2,1,0:T(8,128)(2,1)}, bf16[16,256,256]{2,1,0:T(8,128)(2,1)}, u32[]{:S(2)}, u32[]{:S(2)}) collective-permute-start(bf16[16,256,256]{2,1,0:T(8,128)(2,1)} %bitcast.90), channel_id=1, source_target_pairs={{0,28},{4,0},{8,4},{12,8},{16,12},{20,16},{24,20},{28,24},{1,29},{... | collective-permute-start | bytes 6291464 | tf_op jit(solution)/shard_map/ppermute | solution.py:12
  3.3 47.6 %collective-permute-start = (bf16[16,256,256]{2,1,0:T(8,128)(2,1)}, bf16[16,256,256]{2,1,0:T(8,128)(2,1)}, u32[]{:S(2)}, u32[]{:S(2)}) collective-permute-start(bf16[16,256,256]{2,1,0:T(8,128)(2,1)} %bitcast.92), channel_id=1, source_target_pairs={{0,3},{1,0},{2,1},{3,2},{4,7},{5,4},{6,5},{7,6},{8,11},{9,8},{10,9... | collective-permute-start | bytes 6291464 | tf_op jit(solution)/shard_map/ppermute | solution.py:12
  9.5 4.7 %copy-start = (bf16[1,1,16,256,256]{4,3,2,1,0:T(8,128)(2,1)S(1)}, bf16[1,1,16,256,256]{4,3,2,1,0:T(8,128)(2,1)}, u32[]{:S(2)}) copy-start(bf16[1,1,16,256,256]{4,3,2,1,0:T(8,128)(2,1)} %param.8) | copy-start | bytes 6291460
  27.2 40.1 %collective-permute-start.3 = (bf16[16,256,256]{2,1,0:T(8,128)(2,1)}, bf16[16,256,256]{2,1,0:T(8,128)(2,1)S(1)}, u32[]{:S(2)}, u32[]{:S(2)}) collective-permute-start(bf16[16,256,256]{2,1,0:T(8,128)(2,1)} %collective-permute-done.1), channel_id=1, source_target_pairs={{0,28},{4,0},{8,4},{12,8},{16,12},{20,16},{24,20},{28,24},{1,29},{... | collective-permute-start | bytes 6291464 | tf_op jit(solution)/shard_map/ppermute | solution.py:12
  50.9 47.4 %collective-permute-start.2 = (bf16[16,256,256]{2,1,0:T(8,128)(2,1)}, bf16[16,256,256]{2,1,0:T(8,128)(2,1)}, u32[]{:S(2)}, u32[]{:S(2)}) collective-permute-start(bf16[16,256,256]{2,1,0:T(8,128)(2,1)} %collective-permute-done), channel_id=1, source_target_pairs={{0,3},{1,0},{2,1},{3,2},{4,7},{5,4},{6,5},{7,6},{8,11},{9,8},{10,9... | collective-permute-start | bytes 6291464 | tf_op jit(solution)/shard_map/ppermute | solution.py:12
  67.3 131.6 %collective-permute-start.5 = (bf16[16,256,256]{2,1,0:T(8,128)(2,1)S(1)}, bf16[16,256,256]{2,1,0:T(8,128)(2,1)}, u32[]{:S(2)}, u32[]{:S(2)}) collective-permute-start(bf16[16,256,256]{2,1,0:T(8,128)(2,1)S(1)} %collective-permute-done.3), channel_id=1, source_target_pairs={{0,28},{4,0},{8,4},{12,8},{16,12},{20,16},{24,20},{28,24},{1,29},{... | collective-permute-start | bytes 6291464 | tf_op jit(solution)/shard_map/ppermute | solution.py:12
  98.3 104.9 %collective-permute-start.4 = (bf16[16,256,256]{2,1,0:T(8,128)(2,1)}, bf16[16,256,256]{2,1,0:T(8,128)(2,1)}, u32[]{:S(2)}, u32[]{:S(2)}) collective-permute-start(bf16[16,256,256]{2,1,0:T(8,128)(2,1)} %collective-permute-done.2), channel_id=1, source_target_pairs={{0,3},{1,0},{2,1},{3,2},{4,7},{5,4},{6,5},{7,6},{8,11},{9,8},{10,9... | collective-permute-start | bytes 6291464 | tf_op jit(solution)/shard_map/ppermute | solution.py:12
where the time goes:
time: 245 us; the launch traced here: 244 us
  other arithmetic  86.2 us (35%)
  waiting for transfers between devices  54.4 us (22%)
  local copies, waits for them, and re-layouts  50.6 us (21%)
  matrix products  32.5 us (13%)
  starting transfers between devices  19.8 us (8%)
    scatter-add x4, other arithmetic, accumulate(): return totals.at[slots].add(products, mode='drop')  75.4 us
    ppermute x6, waiting for transfers between devices, shifted(): return lax.ppermute(value, axis, pairs)  54.4 us
    dot_general x4, matrix products, accumulate(): jnp.einsum('pik,pkj->pij', left_blocks[left_pick], right_blocks[right_pic...  32.5 us
    ppermute x6, starting transfers between devices, shifted(): return lax.ppermute(value, axis, pairs)  19.8 us
    gather x4, local copies, waits for them, and re-layouts, accumulate(): right_blocks[right_pick]  16 us
    gather x4, local copies, waits for them, and re-layouts, accumulate(): left_blocks[left_pick]  15.8 us
    broadcast_in_dim x1, other arithmetic, on_device(): return totals.astype(jnp.bfloat16)[None, None]  8.93 us
    broadcast_in_dim x1, local copies, waits for them, and re-layouts, on_device(): totals = jnp.zeros((c_rows.shape[2], block_width, block_width), jnp.float32)  7.77 us
  transfers between devices with their start and end apart: 6, of which 3 were waited for; matrix products, arithmetic and copies ran while one was open for 53% of the time, Pallas kernels for 0%

commit v1 on v0

v1 whole, which is shorter than its diff:
```python
import functools

import jax
import jax.numpy as jnp
from jax import lax
from jax.experimental import pallas as pl
from jax.experimental.pallas import tpu as pltpu
from jax.sharding import PartitionSpec as P

STEPS = 4
MAIN_VMEM = 52 * 2**20
PIECE_VMEM = 24 * 2**20


def shifted(value, axis, steps):
    count = lax.axis_size(axis)
    pairs = [(source, (source + steps) % count) for source in range(count)]
    return lax.ppermute(value, axis, pairs)


def main_kernel(routes, pieces, flag_ref, pick_ref, slot_ref, *refs):
    count = len(pieces)
    sources, refs = refs[: len(routes)], refs[len(routes) :]
    rights, refs = refs[: 2 * STEPS], refs[2 * STEPS :]
    out_ref, part_refs, held_refs = refs[0], refs[1 : 1 + count], refs[1 + count : 1 + 2 * count]
    lefts, right_all, totals, staged, left_sem, right_sem, out_sem, part_sem, held_sem = refs[
        1 + 2 * count :
    ]
    blocks = rights[0].shape[0]
    slots = totals.shape[0]
    flag, odd = flag_ref[0], flag_ref[1]

    def left_copy(place):
        _, start, size, _ = routes[place]
        return pltpu.make_async_copy(
            sources[place], lefts.at[pl.ds(start, size)], left_sem.at[place]
        )

    def when_used(place, action):
        wanted = routes[place][3]
        if wanted is None:
            action()
        else:
            pl.when(flag == wanted)(action)

    def right_copy(step, side):
        return pltpu.make_async_copy(
            rights[2 * step + side],
            right_all.at[pl.ds(step * blocks, blocks)],
            right_sem.at[step],
        )

    for step in range(STEPS):
        for side in range(2):
            pl.when(odd == side)(right_copy(step, side).start)
        for place, route in enumerate(routes):
            if route[0] == step:
                when_used(place, lambda place=place: left_copy(place).start())

    @pl.loop(0, slots)
    def _(slot):
        totals[slot] = jnp.zeros(totals.shape[1:], totals.dtype)

    for step in range(STEPS):
        right_copy(step, 0).wait()

    first_held = 2 * (STEPS - 1) * blocks
    tails = []
    for piece, size in enumerate(pieces):
        tails += [(piece, place) for place in range(2 * size)]

    def held_copy(pair):
        piece, place = tails[pair]
        return pltpu.make_async_copy(
            right_all.at[pick_ref[first_held + pair]],
            held_refs[piece].at[place],
            held_sem.at[pair],
        )

    def part_copy(pair):
        piece, place = tails[pair]
        return pltpu.make_async_copy(
            totals.at[slot_ref[first_held + pair]],
            part_refs[piece].at[place],
            part_sem.at[pair],
        )

    def out_copy(slot):
        return pltpu.make_async_copy(staged.at[slot], out_ref.at[slot], out_sem.at[slot])

    for pair in range(len(tails)):
        held_copy(pair).start()
    for step in range(STEPS - 1):
        for place, route in enumerate(routes):
            if route[0] == step:
                when_used(place, lambda place=place: left_copy(place).wait())

        @pl.loop(step * blocks, (step + 1) * blocks)
        def _(left):
            for side in range(2):
                totals[slot_ref[2 * left + side]] += jnp.dot(
                    lefts[left],
                    right_all[pick_ref[2 * left + side]],
                    preferred_element_type=jnp.float32,
                )

    for pair in range(len(tails)):
        part_copy(pair).start()

    @pl.loop(0, slots)
    def _(slot):
        staged[slot] = totals[slot].astype(staged.dtype)
        out_copy(slot).start()

    @pl.loop(0, slots)
    def _(slot):
        out_copy(slot).wait()

    for pair in range(len(tails)):
        part_copy(pair).wait()
        held_copy(pair).wait()


def main_call(routes, pieces, flag, picks, slots, sources, rights, slot_count):
    rights = [value for pair in rights for value in pair]
    blocks, width = rights[0].shape[0], rights[0].shape[1]
    dtype = rights[0].dtype
    smem = pl.BlockSpec(memory_space=pltpu.SMEM)
    hbm = pl.BlockSpec(memory_space=pl.ANY)
    kept = (STEPS - 1) * blocks
    result = pl.pallas_call(
        functools.partial(main_kernel, routes, pieces),
        out_shape=(
            jax.ShapeDtypeStruct((slot_count, width, width), dtype),
            *[jax.ShapeDtypeStruct((2 * size, width, width), jnp.float32) for size in pieces],
            *[jax.ShapeDtypeStruct((2 * size, width, width), dtype) for size in pieces],
        ),
        in_specs=[smem] * 3 + [hbm] * (len(sources) + 2 * STEPS),
        out_specs=(hbm,) * (1 + 2 * len(pieces)),
        scratch_shapes=[
            pltpu.VMEM((kept, width, width), dtype),
            pltpu.VMEM((STEPS * blocks, width, width), dtype),
            pltpu.VMEM((slot_count, width, width), jnp.float32),
            pltpu.VMEM((slot_count, width, width), dtype),
            pltpu.SemaphoreType.DMA((len(sources),)),
            pltpu.SemaphoreType.DMA((STEPS,)),
            pltpu.SemaphoreType.DMA((slot_count,)),
            pltpu.SemaphoreType.DMA((2 * blocks,)),
            pltpu.SemaphoreType.DMA((2 * blocks,)),
        ],
        compiler_params=pltpu.CompilerParams(vmem_limit_bytes=MAIN_VMEM),
        cost_estimate=pl.CostEstimate(
            flops=4 * kept * width**3,
            bytes_accessed=2 * width * width * (2 * STEPS * blocks + slot_count + 6 * blocks),
            transcendentals=0,
        ),
        name="first_panels",
    )(flag, picks, slots, *sources, *rights)
    return result[0], list(result[1 : 1 + len(pieces)]), list(result[1 + len(pieces) :])


def piece_kernel(choices, later, flag_ref, slot_ref, lead_ref, link_ref, *refs):
    lasts, refs = refs[:choices], refs[choices:]
    part_hbm, held_hbm, refs = refs[0], refs[1], refs[3 + len(later) :]
    out_ref, later_refs, refs = refs[0], refs[1 : 1 + len(later)], refs[1 + len(later) :]
    left, part, held, staged, in_sem, out_sem, later_sem = refs
    pairs = part.shape[0]
    held_copy = pltpu.make_async_copy(held_hbm, held, in_sem.at[0])
    part_copy = pltpu.make_async_copy(part_hbm, part, in_sem.at[1])
    left_copies = [pltpu.make_async_copy(last, left, in_sem.at[2]) for last in lasts]
    for place, copy in enumerate(left_copies):
        pl.when(flag_ref[0] == place)(copy.start)
    held_copy.start()
    part_copy.start()
    left_copies[0].wait()
    held_copy.wait()
    part_copy.wait()
    for pair in range(pairs):
        part[lead_ref[pair]] += jnp.dot(
            left[pair // 2], held[pair], preferred_element_type=jnp.float32
        )

    def out_copy(pair):
        return pltpu.make_async_copy(
            staged.at[pair], out_ref.at[slot_ref[pair]], out_sem.at[pair]
        )

    tails = []
    for piece, size in enumerate(later):
        tails += [(piece, place) for place in range(2 * size)]

    def later_copy(pair):
        piece, place = tails[pair]
        return pltpu.make_async_copy(
            part.at[link_ref[pair]], later_refs[piece].at[place], later_sem.at[pair]
        )

    for pair in range(pairs):

        @pl.when(lead_ref[pair] == pair)
        def _():
            staged[pair] = part[pair].astype(staged.dtype)
            out_copy(pair).start()

    for pair in range(len(tails)):
        pl.when(link_ref[pair] >= 0)(lambda pair=pair: later_copy(pair).start())
    for pair in range(pairs):
        pl.when(lead_ref[pair] == pair)(lambda pair=pair: out_copy(pair).wait())
    for pair in range(len(tails)):
        pl.when(link_ref[pair] >= 0)(lambda pair=pair: later_copy(pair).wait())


def piece_call(flag, slots, leads, links, lasts, part, held, out, later_parts):
    smem = pl.BlockSpec(memory_space=pltpu.SMEM)
    hbm = pl.BlockSpec(memory_space=pl.ANY)
    pairs, width = held.shape[0], held.shape[1]
    later = [value.shape[0] // 2 for value in later_parts]
    first_alias = 4 + len(lasts) + 2
    result = pl.pallas_call(
        functools.partial(piece_kernel, len(lasts), later),
        out_shape=tuple(
            jax.ShapeDtypeStruct(value.shape, value.dtype) for value in (out, *later_parts)
        ),
        in_specs=[smem] * 4 + [hbm] * (len(lasts) + 3 + len(later)),
        out_specs=(hbm,) * (1 + len(later)),
        input_output_aliases={first_alias + place: place for place in range(1 + len(later))},
        scratch_shapes=[
            pltpu.VMEM(lasts[0].shape, lasts[0].dtype),
            pltpu.VMEM(part.shape, part.dtype),
            pltpu.VMEM(held.shape, held.dtype),
            pltpu.VMEM(held.shape, held.dtype),
            pltpu.SemaphoreType.DMA((3,)),
            pltpu.SemaphoreType.DMA((pairs,)),
            pltpu.SemaphoreType.DMA((max(1, 2 * sum(later)),)),
        ],
        compiler_params=pltpu.CompilerParams(vmem_limit_bytes=PIECE_VMEM),
        cost_estimate=pl.CostEstimate(
            flops=2 * pairs * width**3,
            bytes_accessed=2 * width * width * 5 * pairs,
            transcendentals=0,
        ),
        name="last_panel_piece",
    )(flag, slots, leads, links, *lasts, part, held, out, *later_parts)
    return result[0], list(result[1:])


def cut(value, sizes):
    starts = [sum(sizes[:place]) for place in range(len(sizes))]
    return [value[start : start + size] for start, size in zip(starts, sizes)]


def after(value, *others):
    return lax.optimization_barrier((value, *others))[0]


def line_of_four(left, far_sizes):
    me = lax.axis_index("col")
    blocks = left.shape[0]
    cross, out = [(1, 2), (2, 1)], [(2, 3), (1, 0)]
    near = lax.ppermute(left, "col", [(0, 1), (1, 0), (2, 3), (3, 2)])
    mid_in = lax.ppermute(left, "col", cross)
    mid_out = lax.ppermute(mid_in, "col", out)
    far_in = [lax.ppermute(piece, "col", cross) for piece in cut(near, far_sizes)]
    far_out = [lax.ppermute(piece, "col", out) for piece in far_in]
    low = me < 2
    columns = jnp.stack([me, me ^ 1, jnp.where(low, 2, 1), jnp.where(low, 3, 0)])
    at_end = (me == 0) | (me == 3)
    routes = [(0, 0, blocks, None), (1, blocks, blocks, None)]
    routes += [(2, 2 * blocks, blocks, 0), (2, 2 * blocks, blocks, 1)]
    arrays = [left, near, mid_in, mid_out]
    return columns, routes, arrays, list(zip(far_in, far_out)), at_end


def ring(left, far_sizes):
    me, count = lax.axis_index("col"), lax.axis_size("col")
    blocks = left.shape[0]
    near = shifted(left, "col", -1)
    mid = shifted(near, "col", -1)
    far = [shifted(piece, "col", -1) for piece in cut(mid, far_sizes)]
    columns = (me + jnp.arange(STEPS, dtype=jnp.int32)) % count
    routes = [(step, step * blocks, blocks, None) for step in range(STEPS - 1)]
    return columns, routes, [left, near, mid], [(piece,) for piece in far], me < 0


def right_panels(right, behind):
    count = lax.axis_size("row")
    own = lax.ppermute(right, "row", [(row + 1, row) for row in range(0, count, 2)])
    two = shifted(right, "row", -2)
    three = lax.ppermute(
        right, "row", [((row + 3) % count, row) for row in range(1, count, 2)]
    )
    swapped = lax.ppermute(after(two, behind), "row", [(row, row ^ 1) for row in range(count)])
    return [(own, swapped), (two, two), (swapped, three)]


def pair_tables(columns, a_rows, a_inner, b_inner, b_cols, own_rows, own_cols):
    row_id, col_id = lax.axis_index("row"), lax.axis_index("col")
    row_count, col_count = lax.axis_size("row"), lax.axis_size("col")
    steps = (columns - col_id + col_count) % col_count
    left_rows, left_inner = a_rows[row_id][columns], a_inner[row_id][columns]
    right_rows = (row_id + steps) % row_count
    right_inner = b_inner[:, col_id][right_rows]
    right_cols = b_cols[:, col_id][right_rows]
    count = right_inner.shape[1]
    places = jnp.arange(count, dtype=jnp.int32)
    matches = left_inner[:, :, None] == right_inner[:, None, :]
    first = jnp.min(jnp.where(matches, places, count - 1), axis=2)
    second = jnp.max(jnp.where(matches, places, 0), axis=2)
    picks = jnp.stack([first, second], axis=2)
    pair_cols = jnp.sum(
        jnp.where(picks[..., None] == places, right_cols[:, None, None, :], 0), axis=3
    )
    hits = (left_rows[:, :, None, None] == own_rows) & (pair_cols[..., None] == own_cols)
    slot_places = jnp.arange(own_rows.shape[0], dtype=jnp.int32)
    slots = jnp.sum(jnp.where(hits, slot_places, 0), axis=3)
    picks = picks + (steps * count)[:, None, None]
    return picks.reshape(-1).astype(jnp.int32), slots.reshape(-1).astype(jnp.int32)


def on_device(a_panels, b_panels, a_rows, a_inner, b_inner, b_cols, c_rows, c_cols):
    row_id, col_id = lax.axis_index("row"), lax.axis_index("col")
    left, right = a_panels[0, 0], b_panels[0, 0]
    own_rows, own_cols = c_rows[row_id, col_id], c_cols[row_id, col_id]
    gather = line_of_four if lax.axis_size("col") == STEPS else ring
    quarter = left.shape[0] // 4
    rest = left.shape[0] - quarter
    far_sizes = (rest - quarter, quarter, quarter)
    columns, routes, sources, lasts, at_end = gather(left, far_sizes)
    rights = [(right, right), *right_panels(right, lasts[0][0])]
    picks, slots = pair_tables(columns, a_rows, a_inner, b_inner, b_cols, own_rows, own_cols)
    flag = jnp.stack([at_end.astype(jnp.int32), row_id % 2])
    out, parts, helds = main_call(
        routes, far_sizes, flag, picks, slots, sources, rights, c_rows.shape[2]
    )
    piece_slots = cut(slots[-2 * left.shape[0] :], [2 * size for size in far_sizes])
    for place, here in enumerate(piece_slots):
        places = jnp.arange(here.shape[0], dtype=jnp.int32)

        def lead(wanted, other):
            found = jnp.where(wanted[:, None] == here[None, :], places[None, :], here.shape[0])
            first = jnp.min(found, axis=1)
            return jnp.where(first < here.shape[0], first, other)

        leads = lead(here, 0)
        links = lead(jnp.concatenate([*piece_slots[place + 1 :], here[:1]]), -1)
        out, later = piece_call(
            flag, here, leads, links, lasts[place], parts[place], helds[place], out, parts[place + 1 :]
        )
        parts[place + 1 :] = later
    return out[None, None]


def solution(mesh):
    in_specs = (
        P("row", "col", None, None, None),
        P("row", "col", None, None, None),
        P(),
        P(),
        P(),
        P(),
        P(),
        P(),
    )
    out_specs = P("row", "col", None, None, None)
    return jax.shard_map(
        on_device, mesh=mesh, in_specs=in_specs, out_specs=out_specs, check_vma=False
    )
```

time: 245 us -> 159 us (0.65)
  other arithmetic: 86.2 us -> 3.03 us
  Pallas kernels: 0 us -> 34.9 us
  matrix products: 32.5 us -> 0 us
  local copies, waits for them, and re-layouts: 50.6 us -> 22.4 us
  waiting for transfers between devices: 54.4 us -> 77.7 us
    ppermute x0 -> x12, waiting for transfers between devices: none -> 77.7 us  [the longest x1 43.2 us: line_of_four(): mid_out = lax.ppermute(mid_in, 'col', out)]
    scatter-add x4 -> x0, other arithmetic: 75.4 us -> none  [accumulate(): return totals.at[slots].add(products, mode='drop')]
    ppermute x6 -> x1, waiting for transfers between devices: 54.4 us -> 0.01 us  [shifted(): return lax.ppermute(value, axis, pairs)]
    gather x16 -> x4, local copies, waits for them, and re-layouts: 37.4 us -> 2.23 us  [the longest x2 1.11 us: pair_tables(): left_rows, left_inner = (a_rows[row_id][columns], a_inner[row_id][columns])]
    pallas_call x0 -> x4, Pallas kernels: none -> 34.9 us  [the longest x1 25.2 us: main_call(): pl.pallas_call(functools.partial(main_kernel, routes, pieces), out_shape=...]
    dot_general x4 -> x0, matrix products: 32.5 us -> none  [accumulate(): jnp.einsum('pik,pkj->pij', left_blocks[left_pick], right_blocks[right_pic...]
    ppermute x6 -> x1, starting transfers between devices: 19.8 us -> 2.45 us  [shifted(): return lax.ppermute(value, axis, pairs)]
    ppermute x0 -> x12, starting transfers between devices: none -> 16.2 us  [the longest x3 3.87 us: line_of_four(): far_out = [lax.ppermute(piece, 'col', out) for piece in far_in]]
  transfers between devices with their start and end apart: 6 -> 13, of which waited for: 3 -> 2; matrix products, arithmetic and copies ran while one was open for 53% -> 6% of each run, Pallas kernels for 0% -> 20%
where the time goes in v1:
time: 159 us; the launch traced here: 158 us
  waiting for transfers between devices  77.7 us (49%)
  Pallas kernels  34.9 us (22%)
  local copies, waits for them, and re-layouts  22.4 us (14%)
  starting transfers between devices  18.7 us (12%)
  other arithmetic  3.03 us (2%)
    ppermute x1, waiting for transfers between devices, line_of_four(): mid_out = lax.ppermute(mid_in, 'col', out)  43.2 us
    ppermute x1, waiting for transfers between devices, line_of_four(): near = lax.ppermute(left, 'col', [(0, 1), (1, 0), (2, 3), (3, 2)])  34.4 us
    pallas_call x1, Pallas kernels, main_call(): pl.pallas_call(functools.partial(main_kernel, routes, pieces), out_shape=...  25.2 us
    unnamed x24, local copies, waits for them, and re-layouts  15.7 us
    pallas_call x3, Pallas kernels, piece_call(): pl.pallas_call(functools.partial(piece_kernel, len(lasts), later), out_sh...  9.72 us
    ppermute x3, starting transfers between devices, line_of_four(): far_out = [lax.ppermute(piece, 'col', out) for piece in far_in]  3.87 us
  transfers between devices with their start and end apart: 13, of which 2 were waited for; matrix products, arithmetic and copies ran while one was open for 6% of the time, Pallas kernels for 20%

profile of v1, /device:TPU:0, one launch (start us, length us, event | category | flops | bytes accessed | tf_op | source)
XLA Modules:
  0.0 158.1 jit_solution(2973897503314246092)
XLA Ops:
  0.0 3.0 %collective-permute-start = (bf16[16,256,256]{2,1,0:T(8,128)(2,1)}, bf16[16,256,256]{2,1,0:T(8,128)(2,1)S(1)}, u32[]{:S(2)}, u32[]{:S(2)}) collective-permute-start(bf16[16,256,256]{2,1,0:T(8,128)(2,1)} %bitcast.46), channel_id=1, source_target_pairs={{0,1},{1,0},{2,3},{3,2},{4,5},{5,4},{6,7},{7,6},{8,9},{9,8},{10,11... | collective-permute-start | bytes 6291464 | tf_op jit(solution)/shard_map/ppermute | solution.py:260
  3.0 2.0 %collective-permute-start.7 = (bf16[16,256,256]{2,1,0:T(8,128)(2,1)}, bf16[16,256,256]{2,1,0:T(8,128)(2,1)}, u32[]{:S(2)}, u32[]{:S(2)}) collective-permute-start(bf16[16,256,256]{2,1,0:T(8,128)(2,1)} %bitcast.47), channel_id=1, source_target_pairs={{1,2},{2,1},{5,6},{6,5},{9,10},{10,9},{13,14},{14,13},{17,18},{18,... | collective-permute-start | bytes 6291464 | tf_op jit(solution)/shard_map/ppermute | solution.py:261
  5.0 2.4 %collective-permute-start.10 = (bf16[16,256,256]{2,1,0:T(8,128)(2,1)}, bf16[16,256,256]{2,1,0:T(8,128)(2,1)}, u32[]{:S(2)}, u32[]{:S(2)}) collective-permute-start(bf16[16,256,256]{2,1,0:T(8,128)(2,1)} %bitcast.41), channel_id=1, source_target_pairs={{0,24},{4,28},{8,0},{12,4},{16,8},{20,12},{24,16},{28,20},{1,25},{... | collective-permute-start | bytes 6291464 | tf_op jit(solution)/shard_map/ppermute | solution.py:18
  7.4 2.6 %collective-permute-start.12 = (bf16[16,256,256]{2,1,0:T(8,128)(2,1)}, bf16[16,256,256]{2,1,0:T(8,128)(2,1)}, u32[]{:S(2)}, u32[]{:S(2)}) collective-permute-start(bf16[16,256,256]{2,1,0:T(8,128)(2,1)} %bitcast.42), channel_id=1, source_target_pairs={{16,4},{24,12},{0,20},{8,28},{17,5},{25,13},{1,21},{9,29},{18,6},{... | collective-permute-start | bytes 6291464 | tf_op jit(solution)/shard_map/ppermute | solution.py:289
  10.1 1.3 collective-permute-start.9
  11.5 0.8 constant_dynamic-slice_fusion.1
  12.2 0.6 gather_fusion.2
  12.8 0.7 dynamic-slice_bitcast_fusion
  13.5 0.6 gather_fusion.1
  14.2 0.3 fusion
  14.5 34.4 %collective-permute-done.refs_1_ = bf16[16,256,256]{2,1,0:T(8,128)(2,1)S(1)} collective-permute-done((bf16[16,256,256]{2,1,0:T(8,128)(2,1)}, bf16[16,256,256]{2,1,0:T(8,128)(2,1)S(1)}, u32[]{:S(2)}, u32[]{:S(2)}) %collective-permute-start) | collective-permute-done | bytes 2097184 | tf_op jit(solution)/shard_map/ppermute | solution.py:260
  48.9 1.1 slice.66
  50.0 0.7 collective-permute-start.5
  50.8 0.6 gather_fusion.3
  51.3 0.3 select_reduce_fusion.1
  51.6 0.7 fusion.3
  52.3 0.6 gather_fusion
  53.0 0.3 select_reduce_fusion
  53.5 0.7 fusion.14
  54.6 0.1 pad_add_fusion.4
  54.7 1.3 collective-permute-start.8
  56.1 0.1 pad_add_fusion.3
  56.2 0.2 select_reduce_fusion.3
  56.4 0.2 select_reduce_fusion.5
  56.6 0.2 select_reduce_fusion.6
  57.0 0.7 collective-permute-start.3
  57.7 0.7 collective-permute-start.1
  58.5 1.3 collective-permute-start.6
  59.8 1.3 collective-permute-start.4
  61.1 1.3 collective-permute-start.2
  62.4 0.1 copy.30
  62.6 0.1 reshape.408.slot_ref
  62.8 0.1 add.130.pick_ref
  64.1 43.2 %collective-permute-done.8.refs_3_ = bf16[16,256,256]{2,1,0:T(8,128)(2,1)} collective-permute-done((bf16[16,256,256]{2,1,0:T(8,128)(2,1)}, bf16[16,256,256]{2,1,0:T(8,128)(2,1)}, u32[]{:S(2)}, u32[]{:S(2)}) %collective-permute-start.8) | collective-permute-done | bytes 2097184 | tf_op jit(solution)/shard_map/ppermute | solution.py:262
  107.4 25.2 %first_panels.1 = (bf16[64,256,256]{2,1,0:T(8,128)(2,1)}, f32[16,256,256]{2,1,0:T(8,128)}, f32[8,256,256]{2,1,0:T(8,128)}, f32[8,256,256]{2,1,0:T(8,128)}, bf16[...) custom-call(s32[2]{0:T(128)S(1)} %pad_add_fusion.1.flag_ref, ...), custom_call_target="tpu_custom_call" | custom-call | flops 3221225472 | bytes 37748736 | tf_op jit(solution)/shard_map/first_panels/pallas_call | solution.py:131
  132.6 1.6 %copy-done = f32[8,256,256]{2,1,0:T(8,128)S(1)} copy-done((f32[8,256,256]{2,1,0:T(8,128)S(1)}, f32[8,256,256]{2,1,0:T(8,128)}, u32[]{:S(2)}) %copy-start) | copy-done | bytes 2097176
  134.2 1.6 %copy-done.5 = f32[8,256,256]{2,1,0:T(8,128)S(1)} copy-done((f32[8,256,256]{2,1,0:T(8,128)S(1)}, f32[8,256,256]{2,1,0:T(8,128)}, u32[]{:S(2)}) %copy-start.5) | copy-done | bytes 2097176
  135.8 2.2 %copy-done.8 = f32[16,256,256]{2,1,0:T(8,128)S(1)} copy-done((f32[16,256,256]{2,1,0:T(8,128)S(1)}, f32[16,256,256]{2,1,0:T(8,128)}, u32[]{:S(2)}) %copy-start.8) | copy-done | bytes 4194328
  138.0 1.6 %copy-done.9 = bf16[16,256,256]{2,1,0:T(8,128)(2,1)S(1)} copy-done((bf16[16,256,256]{2,1,0:T(8,128)(2,1)S(1)}, bf16[16,256,256]{2,1,0:T(8,128)(2,1)}, u32[]{:S(2)}) %copy-start.9) | copy-done | bytes 2097176
  139.6 3.4 %last_panel_piece.3 = (bf16[64,256,256]{2,1,0:T(8,128)(2,1)}, f32[8,256,256]{2,1,0:T(8,128)S(1)}, f32[8,256,256]{2,1,0:T(8,128)S(1)}) custom-call(s32[2]{0:T(128)S(1)} %pad_add_fusion.1.flag_ref, s32[16]{0:T(128)S(1)} %slice.50.slot_ref, s32[16]{0:T(128)S(1)} %compare_select_fusion.3.lead_ref, ...), custom_call_target="tpu_custom_call", output_to_operand_aliasing={{0}: (8, {}), {1}: (9, {}), {2}: (10, {})} | custom-call | flops 536870912 | bytes 10485760 | tf_op jit(solution)/shard_map/last_panel_piece/pallas_call | solution.py:219
  143.0 1.3 copy-done.1
  144.3 1.4 copy-done.6
  145.6 1.6 %copy-done.2 = f32[8,256,256]{2,1,0:T(8,128)S(1)} copy-done((f32[8,256,256]{2,1,0:T(8,128)S(1)}, f32[8,256,256]{2,1,0:T(8,128)}, u32[]{:S(2)}) %copy-start.2) | copy-done | bytes 2097176
  147.2 1.6 %copy-done.7 = f32[8,256,256]{2,1,0:T(8,128)S(1)} copy-done((f32[8,256,256]{2,1,0:T(8,128)S(1)}, f32[8,256,256]{2,1,0:T(8,128)}, u32[]{:S(2)}) %copy-start.7) | copy-done | bytes 2097176
  148.8 3.2 %last_panel_piece.4 = (bf16[64,256,256]{2,1,0:T(8,128)(2,1)}, f32[8,256,256]{2,1,0:T(8,128)S(1)}) custom-call(s32[2]{0:T(128)S(1)} %pad_add_fusion.1.flag_ref, s32[8]{0:T(128)S(1)} %slice.46.slot_ref, s32[8]{0:T(128)S(1)} %compare_select_fusion.5.lead_ref, s32[9]{0:T(128)S(1)} %compare_select_fusion.4.link_ref, ...), custom_call_target="tpu_custom_call", output_to_operand_aliasing={{0}: (8, {}), {1}: (9, {})} | custom-call | flops 268435456 | bytes 5242880 | tf_op jit(solution)/shard_map/last_panel_piece/pallas_call | solution.py:219
  152.0 1.3 copy-done.3
  153.4 1.6 %copy-done.4 = f32[8,256,256]{2,1,0:T(8,128)S(1)} copy-done((f32[8,256,256]{2,1,0:T(8,128)S(1)}, f32[8,256,256]{2,1,0:T(8,128)}, u32[]{:S(2)}) %copy-start.4) | copy-done | bytes 2097176
  155.0 3.1 %last_panel_piece.5 = bf16[64,256,256]{2,1,0:T(8,128)(2,1)} custom-call(s32[2]{0:T(128)S(1)} %pad_add_fusion.1.flag_ref, s32[8]{0:T(128)S(1)} %slice.42.slot_ref, s32[8]{0:T(128)S(1)} %compare_select_fusion.6.lead_ref, s32[1]{0:T(128)S(6)} %select_n.158.link_ref, ...), custom_call_target="tpu_custom_call", output_to_operand_aliasing={{}: (8, {})} | custom-call | flops 268435456 | bytes 5242880 | tf_op jit(solution)/shard_map/last_panel_piece/pallas_call | solution.py:219
  (52 shorter events, 1.5 us)
Async XLA Ops:
  0.0 48.9 %collective-permute-start = (bf16[16,256,256]{2,1,0:T(8,128)(2,1)}, bf16[16,256,256]{2,1,0:T(8,128)(2,1)S(1)}, u32[]{:S(2)}, u32[]{:S(2)}) collective-permute-start(bf16[16,256,256]{2,1,0:T(8,128)(2,1)} %bitcast.46), channel_id=1, source_target_pairs={{0,1},{1,0},{2,3},{3,2},{4,5},{5,4},{6,7},{7,6},{8,9},{9,8},{10,11... | collective-permute-start | bytes 6291464 | tf_op jit(solution)/shard_map/ppermute | solution.py:260
  3.0 51.7 %collective-permute-start.7 = (bf16[16,256,256]{2,1,0:T(8,128)(2,1)}, bf16[16,256,256]{2,1,0:T(8,128)(2,1)}, u32[]{:S(2)}, u32[]{:S(2)}) collective-permute-start(bf16[16,256,256]{2,1,0:T(8,128)(2,1)} %bitcast.47), channel_id=1, source_target_pairs={{1,2},{2,1},{5,6},{6,5},{9,10},{10,9},{13,14},{14,13},{17,18},{18,... | collective-permute-start | bytes 6291464 | tf_op jit(solution)/shard_map/ppermute | solution.py:261
  5.0 51.0 %collective-permute-start.10 = (bf16[16,256,256]{2,1,0:T(8,128)(2,1)}, bf16[16,256,256]{2,1,0:T(8,128)(2,1)}, u32[]{:S(2)}, u32[]{:S(2)}) collective-permute-start(bf16[16,256,256]{2,1,0:T(8,128)(2,1)} %bitcast.41), channel_id=1, source_target_pairs={{0,24},{4,28},{8,0},{12,4},{16,8},{20,12},{24,16},{28,20},{1,25},{... | collective-permute-start | bytes 6291464 | tf_op jit(solution)/shard_map/ppermute | solution.py:18
  7.4 50.3 %collective-permute-start.12 = (bf16[16,256,256]{2,1,0:T(8,128)(2,1)}, bf16[16,256,256]{2,1,0:T(8,128)(2,1)}, u32[]{:S(2)}, u32[]{:S(2)}) collective-permute-start(bf16[16,256,256]{2,1,0:T(8,128)(2,1)} %bitcast.42), channel_id=1, source_target_pairs={{16,4},{24,12},{0,20},{8,28},{17,5},{25,13},{1,21},{9,29},{18,6},{... | collective-permute-start | bytes 6291464 | tf_op jit(solution)/shard_map/ppermute | solution.py:289
  10.1 48.4 %collective-permute-start.9 = (bf16[16,256,256]{2,1,0:T(8,128)(2,1)}, bf16[16,256,256]{2,1,0:T(8,128)(2,1)}, u32[]{:S(2)}, u32[]{:S(2)}) collective-permute-start(bf16[16,256,256]{2,1,0:T(8,128)(2,1)} %bitcast.43), channel_id=1, source_target_pairs={{4,0},{12,8},{20,16},{28,24},{5,1},{13,9},{21,17},{29,25},{6,2},{1... | collective-permute-start | bytes 6291464 | tf_op jit(solution)/shard_map/ppermute | solution.py:287
  48.9 8.1 %copy-start.11 = (bf16[16,256,256]{2,1,0:T(8,128)(2,1)}, bf16[16,256,256]{2,1,0:T(8,128)(2,1)S(1)}, u32[]{:S(2)}) copy-start(bf16[16,256,256]{2,1,0:T(8,128)(2,1)S(1)} %collective-permute-done.refs_1_) | copy-start | bytes 6291460
  50.0 6.1 %collective-permute-start.5 = (bf16[8,256,256]{2,1,0:T(8,128)(2,1)}, bf16[8,256,256]{2,1,0:T(8,128)(2,1)S(1)}, u32[]{:S(2)}, u32[]{:S(2)}) collective-permute-start(bf16[8,256,256]{2,1,0:T(8,128)(2,1)} %slice.66), channel_id=1, source_target_pairs={{1,2},{2,1},{5,6},{6,5},{9,10},{10,9},{13,14},{14,13},{17,18},{18,... | collective-permute-start | bytes 3145736 | tf_op jit(solution)/shard_map/ppermute | solution.py:263
  54.7 52.6 %collective-permute-start.8 = (bf16[16,256,256]{2,1,0:T(8,128)(2,1)}, bf16[16,256,256]{2,1,0:T(8,128)(2,1)}, u32[]{:S(2)}, u32[]{:S(2)}) collective-permute-start(bf16[16,256,256]{2,1,0:T(8,128)(2,1)} %collective-permute-done.7.refs_2_), channel_id=1, source_target_pairs={{2,3},{1,0},{6,7},{5,4},{10,11},{9,8},{14,15},{13,12},{18,19},{17,... | collective-permute-start | bytes 6291464 | tf_op jit(solution)/shard_map/ppermute | solution.py:262
  56.1 51.3 %collective-permute-start.11 = (bf16[16,256,256]{2,1,0:T(8,128)(2,1)}, bf16[16,256,256]{2,1,0:T(8,128)(2,1)}, u32[]{:S(2)}, u32[]{:S(2)}) collective-permute-start(bf16[16,256,256]{2,1,0:T(8,128)(2,1)} %collective-permute-done.10.refs_8_.refs_9_), channel_id=1, source_target_pairs={{0,4},{4,0},{8,12},{12,8},{16,20},{20,16},{24,28},{28,24},{1,5},{5... | collective-permute-start | bytes 6291464 | tf_op jit(solution)/shard_map/ppermute | solution.py:292
  57.0 2.8 %collective-permute-start.3 = (bf16[4,256,256]{2,1,0:T(8,128)(2,1)S(1)}, bf16[4,256,256]{2,1,0:T(8,128)(2,1)S(1)}, u32[]{:S(2)}, u32[]{:S(2)}) collective-permute-start(bf16[4,256,256]{2,1,0:T(8,128)(2,1)S(1)} %get-tuple-element.35), channel_id=1, source_target_pairs={{1,2},{2,1},{5,6},{6,5},{9,10},{10,9},{13,14},{14,13},{17,18},{18,... | collective-permute-start | bytes 1572872 | tf_op jit(solution)/shard_map/ppermute | solution.py:263
  57.7 3.4 %collective-permute-start.1 = (bf16[4,256,256]{2,1,0:T(8,128)(2,1)S(1)}, bf16[4,256,256]{2,1,0:T(8,128)(2,1)S(1)}, u32[]{:S(2)}, u32[]{:S(2)}) collective-permute-start(bf16[4,256,256]{2,1,0:T(8,128)(2,1)S(1)} %get-tuple-element.36), channel_id=1, source_target_pairs={{1,2},{2,1},{5,6},{6,5},{9,10},{10,9},{13,14},{14,13},{17,18},{18,... | collective-permute-start | bytes 1572872 | tf_op jit(solution)/shard_map/ppermute | solution.py:263
  58.5 74.1 %collective-permute-start.6 = (bf16[8,256,256]{2,1,0:T(8,128)(2,1)S(1)}, bf16[8,256,256]{2,1,0:T(8,128)(2,1)S(1)}, u32[]{:S(2)}, u32[]{:S(2)}) collective-permute-start(bf16[8,256,256]{2,1,0:T(8,128)(2,1)S(1)} %collective-permute-done.5.refs_0_), channel_id=1, source_target_pairs={{2,3},{1,0},{6,7},{5,4},{10,11},{9,8},{14,15},{13,12},{18,19},{17,... | collective-permute-start | bytes 3145736 | tf_op jit(solution)/shard_map/ppermute | solution.py:264
  59.8 85.8 %collective-permute-start.4 = (bf16[4,256,256]{2,1,0:T(8,128)(2,1)S(1)}, bf16[4,256,256]{2,1,0:T(8,128)(2,1)}, u32[]{:S(2)}, u32[]{:S(2)}) collective-permute-start(bf16[4,256,256]{2,1,0:T(8,128)(2,1)S(1)} %collective-permute-done.3.refs_0_), channel_id=1, source_target_pairs={{2,3},{1,0},{6,7},{5,4},{10,11},{9,8},{14,15},{13,12},{18,19},{17,... | collective-permute-start | bytes 1572872 | tf_op jit(solution)/shard_map/ppermute | solution.py:264
  61.1 92.2 %collective-permute-start.2 = (bf16[4,256,256]{2,1,0:T(8,128)(2,1)S(1)}, bf16[4,256,256]{2,1,0:T(8,128)(2,1)}, u32[]{:S(2)}, u32[]{:S(2)}) collective-permute-start(bf16[4,256,256]{2,1,0:T(8,128)(2,1)S(1)} %collective-permute-done.1.refs_0_), channel_id=1, source_target_pairs={{2,3},{1,0},{6,7},{5,4},{10,11},{9,8},{14,15},{13,12},{18,19},{17,... | collective-permute-start | bytes 1572872 | tf_op jit(solution)/shard_map/ppermute | solution.py:264
  132.6 1.6 %copy-start = (f32[8,256,256]{2,1,0:T(8,128)S(1)}, f32[8,256,256]{2,1,0:T(8,128)}, u32[]{:S(2)}) copy-start(f32[8,256,256]{2,1,0:T(8,128)} %get-tuple-element.23.refs_6_) | copy-start | bytes 6291460
  134.2 1.6 %copy-start.5 = (f32[8,256,256]{2,1,0:T(8,128)S(1)}, f32[8,256,256]{2,1,0:T(8,128)}, u32[]{:S(2)}) copy-start(f32[8,256,256]{2,1,0:T(8,128)} %get-tuple-element.22.refs_5_) | copy-start | bytes 6291460
  135.8 2.2 %copy-start.8 = (f32[16,256,256]{2,1,0:T(8,128)S(1)}, f32[16,256,256]{2,1,0:T(8,128)}, u32[]{:S(2)}) copy-start(f32[16,256,256]{2,1,0:T(8,128)} %get-tuple-element.19.refs_2_) | copy-start | bytes 12582916
  138.0 1.6 %copy-start.9 = (bf16[16,256,256]{2,1,0:T(8,128)(2,1)S(1)}, bf16[16,256,256]{2,1,0:T(8,128)(2,1)}, u32[]{:S(2)}) copy-start(bf16[16,256,256]{2,1,0:T(8,128)(2,1)} %get-tuple-element.20.refs_3_) | copy-start | bytes 6291460
  143.0 1.3 copy-start.1
  144.3 1.4 copy-start.6
  145.6 1.6 %copy-start.2 = (f32[8,256,256]{2,1,0:T(8,128)S(1)}, f32[8,256,256]{2,1,0:T(8,128)}, u32[]{:S(2)}) copy-start(f32[8,256,256]{2,1,0:T(8,128)} %copy-done.1) | copy-start | bytes 6291460
  147.2 1.6 %copy-start.7 = (f32[8,256,256]{2,1,0:T(8,128)S(1)}, f32[8,256,256]{2,1,0:T(8,128)}, u32[]{:S(2)}) copy-start(f32[8,256,256]{2,1,0:T(8,128)} %copy-done.6) | copy-start | bytes 6291460
  148.8 4.5 %copy-start.10 = (bf16[8,256,256]{2,1,0:T(8,128)(2,1)S(1)}, bf16[8,256,256]{2,1,0:T(8,128)(2,1)}, u32[]{:S(2)}) copy-start(bf16[8,256,256]{2,1,0:T(8,128)(2,1)} %get-tuple-element.29.refs_3_) | copy-start | bytes 3145732
  152.0 1.4 copy-start.3
  153.4 1.6 %copy-start.4 = (f32[8,256,256]{2,1,0:T(8,128)S(1)}, f32[8,256,256]{2,1,0:T(8,128)}, u32[]{:S(2)}) copy-start(f32[8,256,256]{2,1,0:T(8,128)} %copy-done.3) | copy-start | bytes 6291460

commit v2 on v1

v2 whole, which is shorter than its diff:
```python
import functools

import jax
import jax.numpy as jnp
from jax import lax
from jax.experimental import pallas as pl
from jax.experimental.pallas import tpu as pltpu
from jax.sharding import PartitionSpec as P

STEPS = 4
VMEM_BYTES = 60 * 2**20
FINAL_VMEM = 16 * 2**20
UNROLL = 4
SMALL = pl.CostEstimate(flops=2**20, bytes_accessed=2**16, transcendentals=0)


def shifted(value, axis, steps):
    count = lax.axis_size(axis)
    pairs = [(source, (source + steps) % count) for source in range(count)]
    return lax.ppermute(value, axis, pairs)


def main_kernel(routes, takers, pieces, layout, table_ref, *refs):
    count = len(pieces)
    sources, refs = refs[: len(routes)], refs[len(routes) :]
    rights, refs = refs[: len(takers)], refs[len(takers) :]
    out_ref, part_refs, held_refs = refs[0], refs[1 : 1 + count], refs[1 + count : 1 + 2 * count]
    lefts, right_all, totals, staged, left_sem, right_sem, out_sem, part_sem, held_sem = refs[
        1 + 2 * count :
    ]
    blocks = rights[0].shape[0]
    slots = totals.shape[0]
    flag, kind = table_ref[layout["flags"]], table_ref[layout["flags"] + 1]

    def pick_of(pair):
        return table_ref[layout["picks"] + pair]

    def slot_of(pair):
        return table_ref[layout["slots"] + pair]

    def left_copy(place):
        _, start, size, _ = routes[place]
        return pltpu.make_async_copy(
            sources[place], lefts.at[pl.ds(start, size)], left_sem.at[place]
        )

    def when_used(place, action):
        wanted = routes[place][3]
        if wanted is None:
            action()
        else:
            pl.when(flag == wanted)(action)

    def right_copy(place):
        step, start, _ = takers[place]
        return pltpu.make_async_copy(
            rights[place],
            right_all.at[pl.ds(step * blocks + start, rights[place].shape[0])],
            right_sem.at[place],
        )

    def when_taken(step, action):
        for place, (wanted, _, kinds) in enumerate(takers):
            if wanted == step:
                for one in kinds:
                    pl.when(kind == one)(lambda place=place: action(place))

    for step in range(STEPS):
        for place, route in enumerate(routes):
            if route[0] == step:
                when_used(place, lambda place=place: left_copy(place).start())
        when_taken(step, lambda place: right_copy(place).start())

    @pl.loop(0, slots)
    def _(slot):
        totals[slot] = jnp.zeros(totals.shape[1:], totals.dtype)

    first_held = 2 * (STEPS - 1) * blocks
    tails = []
    for piece, size in enumerate(pieces):
        tails += [(piece, place) for place in range(2 * size)]

    def held_copy(pair):
        piece, place = tails[pair]
        return pltpu.make_async_copy(
            right_all.at[pick_of(first_held + pair)],
            held_refs[piece].at[place],
            held_sem.at[pair],
        )

    def part_copy(pair):
        piece, place = tails[pair]
        return pltpu.make_async_copy(
            totals.at[slot_of(first_held + pair)],
            part_refs[piece].at[place],
            part_sem.at[pair],
        )

    def out_copy(slot):
        return pltpu.make_async_copy(staged.at[slot], out_ref.at[slot], out_sem.at[slot])

    for step in range(STEPS - 1):
        for place, route in enumerate(routes):
            if route[0] == step:
                when_used(place, lambda place=place: left_copy(place).wait())
        for other in [(0,), range(1, STEPS), ()][min(step, 2)]:
            when_taken(other, lambda place: right_copy(place).wait())
        if step == 1:
            for pair in range(len(tails)):
                held_copy(pair).start()

        @pl.loop(step * blocks, (step + 1) * blocks, unroll=UNROLL)
        def _(left):
            for side in range(2):
                totals[slot_of(2 * left + side)] += jnp.dot(
                    lefts[left],
                    right_all[pick_of(2 * left + side)],
                    preferred_element_type=jnp.float32,
                )

    for pair in range(len(tails)):
        part_copy(pair).start()

    @pl.loop(0, slots)
    def _(slot):
        staged[slot] = totals[slot].astype(staged.dtype)
        out_copy(slot).start()

    @pl.loop(0, slots)
    def _(slot):
        out_copy(slot).wait()

    for pair in range(len(tails)):
        part_copy(pair).wait()
        held_copy(pair).wait()


def main_call(routes, takers, pieces, layout, table, sources, rights, slot_count):
    blocks, width = rights[0].shape[0], rights[0].shape[1]
    dtype = rights[0].dtype
    smem = pl.BlockSpec(memory_space=pltpu.SMEM)
    hbm = pl.BlockSpec(memory_space=pl.ANY)
    kept = (STEPS - 1) * blocks
    result = pl.pallas_call(
        functools.partial(main_kernel, routes, takers, pieces, layout),
        out_shape=(
            jax.ShapeDtypeStruct((slot_count, width, width), dtype),
            *[jax.ShapeDtypeStruct((2 * size, width, width), jnp.float32) for size in pieces],
            *[jax.ShapeDtypeStruct((2 * size, width, width), dtype) for size in pieces],
        ),
        in_specs=[smem] + [hbm] * (len(sources) + len(rights)),
        out_specs=(hbm,) * (1 + 2 * len(pieces)),
        scratch_shapes=[
            pltpu.VMEM((kept, width, width), dtype),
            pltpu.VMEM((STEPS * blocks, width, width), dtype),
            pltpu.VMEM((slot_count, width, width), jnp.float32),
            pltpu.VMEM((slot_count, width, width), dtype),
            pltpu.SemaphoreType.DMA((len(sources),)),
            pltpu.SemaphoreType.DMA((len(rights),)),
            pltpu.SemaphoreType.DMA((slot_count,)),
            pltpu.SemaphoreType.DMA((2 * blocks,)),
            pltpu.SemaphoreType.DMA((2 * blocks,)),
        ],
        compiler_params=pltpu.CompilerParams(vmem_limit_bytes=VMEM_BYTES),
        cost_estimate=SMALL,
        name="first_panels",
    )(table, *sources, *rights)
    return result[0], list(result[1 : 1 + len(pieces)]), list(result[1 + len(pieces) :])


def piece_kernel(choices, later, layout, number, table_ref, *refs):
    def entry(name, pair):
        return table_ref[layout[name, number] + pair]

    lasts, refs = refs[:choices], refs[choices:]
    part_hbm, held_hbm, refs = refs[0], refs[1], refs[3 + len(later) :]
    out_ref, later_refs, refs = refs[0], refs[1 : 1 + len(later)], refs[1 + len(later) :]
    left, part, held, staged, left_sem, held_sem, part_sem, out_sem, later_sem = refs
    pairs = part.shape[0]

    def left_copy(block, place):
        return pltpu.make_async_copy(
            lasts[place].at[block], left.at[block], left_sem.at[block]
        )

    def held_copy(pair):
        return pltpu.make_async_copy(held_hbm.at[pair], held.at[pair], held_sem.at[pair])

    def part_copy(pair):
        return pltpu.make_async_copy(part_hbm.at[pair], part.at[pair], part_sem.at[pair])

    def out_copy(pair):
        return pltpu.make_async_copy(
            staged.at[pair], out_ref.at[entry("here", pair)], out_sem.at[pair]
        )

    for block in range(pairs // 2):
        for place in range(choices):
            pl.when(table_ref[layout["flags"]] == place)(
                lambda block=block, place=place: left_copy(block, place).start()
            )
        for pair in (2 * block, 2 * block + 1):
            held_copy(pair).start()
            part_copy(pair).start()

    for pair in range(pairs):
        if pair % 2 == 0:
            left_copy(pair // 2, 0).wait()
        held_copy(pair).wait()
        part_copy(pair).wait()
        lead = entry("lead", pair)
        total = part[lead] + jnp.dot(
            left[pair // 2], held[pair], preferred_element_type=jnp.float32
        )
        part[lead] = total
        staged[pair] = total.astype(staged.dtype)
        pl.when(entry("final", pair) == 1)(lambda pair=pair: out_copy(pair).start())

    tails = []
    for piece, size in enumerate(later):
        tails += [(piece, place) for place in range(2 * size)]

    def later_copy(pair):
        piece, place = tails[pair]
        return pltpu.make_async_copy(
            part.at[entry("link", pair)], later_refs[piece].at[place], later_sem.at[pair]
        )

    for pair in range(len(tails)):
        pl.when(entry("link", pair) >= 0)(lambda pair=pair: later_copy(pair).start())
    for pair in range(pairs):
        pl.when(entry("final", pair) == 1)(lambda pair=pair: out_copy(pair).wait())
    for pair in range(len(tails)):
        pl.when(entry("link", pair) >= 0)(lambda pair=pair: later_copy(pair).wait())


def piece_call(layout, number, table, lasts, part, held, out, later_parts):
    smem = pl.BlockSpec(memory_space=pltpu.SMEM)
    hbm = pl.BlockSpec(memory_space=pl.ANY)
    pairs, width = held.shape[0], held.shape[1]
    later = [value.shape[0] // 2 for value in later_parts]
    first_alias = 1 + len(lasts) + 2
    result = pl.pallas_call(
        functools.partial(piece_kernel, len(lasts), later, layout, number),
        out_shape=tuple(
            jax.ShapeDtypeStruct(value.shape, value.dtype) for value in (out, *later_parts)
        ),
        in_specs=[smem] + [hbm] * (len(lasts) + 3 + len(later)),
        out_specs=(hbm,) * (1 + len(later)),
        input_output_aliases={first_alias + place: place for place in range(1 + len(later))},
        scratch_shapes=[
            pltpu.VMEM(lasts[0].shape, lasts[0].dtype),
            pltpu.VMEM(part.shape, part.dtype),
            pltpu.VMEM(held.shape, held.dtype),
            pltpu.VMEM(held.shape, held.dtype),
            pltpu.SemaphoreType.DMA((pairs // 2,)),
            pltpu.SemaphoreType.DMA((pairs,)),
            pltpu.SemaphoreType.DMA((pairs,)),
            pltpu.SemaphoreType.DMA((pairs,)),
            pltpu.SemaphoreType.DMA((max(1, 2 * sum(later)),)),
        ],
        compiler_params=pltpu.CompilerParams(vmem_limit_bytes=VMEM_BYTES),
        cost_estimate=SMALL,
        name="last_panel_piece",
    )(table, *lasts, part, held, out, *later_parts)
    return result[0], list(result[1:])


def final_kernel(choices, layout, number, table_ref, *refs):
    lasts, refs = refs[:choices], refs[choices:]
    part_hbm, held, _, out_ref, part, totals, staged, part_sem, out_sem = refs
    pairs = part.shape[0]
    part_copies = [
        pltpu.make_async_copy(part_hbm.at[pair], part.at[pair], part_sem.at[pair])
        for pair in range(pairs)
    ]
    for copy in part_copies:
        copy.start()

    def entry(name, pair):
        return table_ref[layout[name, number] + pair]

    def out_copy(pair):
        return pltpu.make_async_copy(
            staged.at[pair], out_ref.at[entry("here", pair)], out_sem.at[pair]
        )

    for block in range(pairs // 2):
        left = lasts[0][block]
        for place in range(1, choices):
            left = jnp.where(table_ref[layout["flags"]] == place, lasts[place][block], left)
        for pair in (2 * block, 2 * block + 1):
            lead = entry("lead", pair)
            product = jnp.dot(left, held[pair], preferred_element_type=jnp.float32)
            part_copies[pair].wait()

            @pl.when(lead == pair)
            def _():
                totals[pair] = part[pair] + product

            @pl.when(lead != pair)
            def _():
                totals[lead] += product

            @pl.when(entry("final", pair) == 1)
            def _():
                staged[pair] = totals[lead].astype(staged.dtype)
                out_copy(pair).start()

    for pair in range(pairs):
        pl.when(entry("final", pair) == 1)(lambda pair=pair: out_copy(pair).wait())


def final_call(layout, number, table, lasts, part, held, out):
    smem = pl.BlockSpec(memory_space=pltpu.SMEM)
    vmem = pl.BlockSpec(memory_space=pltpu.VMEM)
    hbm = pl.BlockSpec(memory_space=pl.ANY)
    pinned = pl.BlockSpec(memory_space=pltpu.HBM)
    pairs, width = held.shape[0], held.shape[1]
    return pl.pallas_call(
        functools.partial(final_kernel, len(lasts), layout, number),
        out_shape=jax.ShapeDtypeStruct(out.shape, out.dtype),
        in_specs=[smem] + [vmem] * len(lasts) + [pinned, vmem, hbm],
        out_specs=hbm,
        input_output_aliases={len(lasts) + 3: 0},
        scratch_shapes=[
            pltpu.VMEM(part.shape, part.dtype),
            pltpu.VMEM(part.shape, part.dtype),
            pltpu.VMEM(held.shape, held.dtype),
            pltpu.SemaphoreType.DMA((pairs,)),
            pltpu.SemaphoreType.DMA((pairs,)),
        ],
        compiler_params=pltpu.CompilerParams(vmem_limit_bytes=FINAL_VMEM),
        cost_estimate=SMALL,
        name="last_piece",
    )(table, *lasts, part, held, out)


def cut(value, sizes):
    starts = [sum(sizes[:place]) for place in range(len(sizes))]
    return [value[start : start + size] for start, size in zip(starts, sizes)]


def after(value, *others):
    return lax.optimization_barrier((value, *others))[0]


def line_columns(me):
    low = me < 2
    return jnp.stack([me, me ^ 1, jnp.where(low, 2, 1), jnp.where(low, 3, 0)])


def ring_columns(me):
    return (me + jnp.arange(STEPS, dtype=jnp.int32)) % lax.axis_size("col")


def line_of_four(left, far_sizes, early, fetched):
    blocks = left.shape[0]
    cross, out = [(1, 2), (2, 1)], [(2, 3), (1, 0)]
    near = lax.ppermute(left, "col", [(0, 1), (1, 0), (2, 3), (3, 2)])
    mid_in = lax.ppermute(left, "col", cross)
    mid_out = lax.ppermute(mid_in, "col", out)
    near = after(near, mid_in, early)
    far_in = [
        lax.ppermute(after(piece, *fetched) if place == 1 else piece, "col", cross)
        for place, piece in enumerate(cut(near, far_sizes))
    ]
    far_out = [
        lax.ppermute(after(piece, mid_out) if place else piece, "col", out)
        for place, piece in enumerate(far_in)
    ]
    routes = [(0, 0, blocks, None), (1, blocks, blocks, None)]
    routes += [(2, 2 * blocks, blocks, 0), (2, 2 * blocks, blocks, 1)]
    return routes, [left, near, mid_in, mid_out], list(zip(far_in, far_out))


def ring(left, far_sizes, *_):
    blocks = left.shape[0]
    near = shifted(left, "col", -1)
    mid = shifted(near, "col", -1)
    far = [shifted(piece, "col", -1) for piece in cut(mid, far_sizes)]
    routes = [(step, step * blocks, blocks, None) for step in range(STEPS - 1)]
    return routes, [left, near, mid], [(piece,) for piece in far]


def right_panels(right):
    count = lax.axis_size("row")
    rows = range(count)

    def send(value, takers, distance):
        pairs = [((row + distance) % count, row) for row in rows if row % 4 in takers]
        return lax.ppermute(value, "row", pairs)

    own = send(right, (0, 2), 1)
    two = send(right, (0, 1, 2, 3), 2)
    three = send(right, (1, 3), 3)
    return own, two, three


def passed_on(own, two, three):
    half = two.shape[0] // 2
    rows = range(lax.axis_size("row"))
    swap = [(row, row ^ 1) for row in rows]
    passed = [lax.ppermute(part, "row", swap) for part in (two[:half], two[half:])]
    takers = [(1, 0, (0, 2)), (2, 0, (0, 1, 2, 3)), (3, 0, (1, 3))]
    for place in range(2):
        takers += [(1, place * half, (1, 3)), (3, place * half, (0, 2))]
    return takers, [own, two, three, *[part for part in passed for _ in range(2)]]


def pair_tables(columns, a_rows, a_inner, b_inner, b_cols, own_rows, own_cols):
    row_id, col_id = lax.axis_index("row"), lax.axis_index("col")
    row_count, col_count = lax.axis_size("row"), lax.axis_size("col")
    steps = (columns - col_id + col_count) % col_count
    left_rows, left_inner = a_rows[row_id][columns], a_inner[row_id][columns]
    right_rows = (row_id + steps) % row_count
    right_inner = b_inner[:, col_id][right_rows]
    right_cols = b_cols[:, col_id][right_rows]
    count = right_inner.shape[1]
    places = jnp.arange(count, dtype=jnp.int32)
    matches = left_inner[:, :, None] == right_inner[:, None, :]
    first = jnp.min(jnp.where(matches, places, count - 1), axis=2)
    second = jnp.max(jnp.where(matches, places, 0), axis=2)
    picks = jnp.stack([first, second], axis=2)
    pair_cols = jnp.sum(
        jnp.where(picks[..., None] == places, right_cols[:, None, None, :], 0), axis=3
    )
    hits = (left_rows[:, :, None, None] == own_rows) & (pair_cols[..., None] == own_cols)
    slot_places = jnp.arange(own_rows.shape[0], dtype=jnp.int32)
    slots = jnp.sum(jnp.where(hits, slot_places, 0), axis=3)
    picks = picks + (steps * count)[:, None, None]
    return picks.reshape(-1).astype(jnp.int32), slots.reshape(-1).astype(jnp.int32)


def piece_tables(slots, sizes):
    cuts = cut(slots, [2 * size for size in sizes])
    tables = {}
    for number, here in enumerate(cuts):
        count = here.shape[0]
        places = jnp.arange(count, dtype=jnp.int32)

        def lead(wanted):
            same = wanted[:, None] == here[None, :]
            first = jnp.min(jnp.where(same, places[None, :], count), axis=1)
            return jnp.where(first < count, first, -1)

        again = (here[:, None] == here[None, :]) & (places[None, :] > places[:, None])
        tables["here", number] = here
        tables["lead", number] = lead(here)
        tables["final", number] = 1 - jnp.max(again.astype(jnp.int32), axis=1)
        if number + 1 < len(sizes):
            tables["link", number] = lead(jnp.concatenate(cuts[number + 1 :]))
    return tables


def packed(tables):
    starts, total = {}, 0
    for name, value in tables.items():
        starts[name], total = total, total + value.shape[0]
    return jnp.concatenate([value.astype(jnp.int32) for value in tables.values()]), starts


def on_device(a_panels, b_panels, a_rows, a_inner, b_inner, b_cols, c_rows, c_cols):
    row_id, col_id = lax.axis_index("row"), lax.axis_index("col")
    left, right = a_panels[0, 0], b_panels[0, 0]
    own_rows, own_cols = c_rows[row_id, col_id], c_cols[row_id, col_id]
    on_line = lax.axis_size("col") == STEPS
    eighth = left.shape[0] // 8
    far_sizes = (left.shape[0] - 4 * eighth, 3 * eighth, eighth)
    columns = (line_columns if on_line else ring_columns)(col_id)
    picks, slots = pair_tables(columns, a_rows, a_inner, b_inner, b_cols, own_rows, own_cols)
    at_end = on_line & ((col_id == 0) | (col_id == 3))
    flags = jnp.stack([at_end.astype(jnp.int32), row_id % 4])
    pieces = piece_tables(slots[-2 * left.shape[0] :], far_sizes)
    table, layout = packed({"flags": flags, "picks": picks, "slots": slots, **pieces})
    gather = line_of_four if on_line else ring
    fetched = right_panels(right)
    routes, sources, lasts = gather(left, far_sizes, table, fetched)
    takers, rights = passed_on(*fetched)
    out, parts, helds = main_call(
        routes,
        [(0, 0, (0, 1, 2, 3)), *takers],
        far_sizes,
        layout,
        table,
        sources,
        [right, *rights],
        c_rows.shape[2],
    )
    last = len(far_sizes) - 1
    for number in range(last):
        out, parts[number + 1 :] = piece_call(
            layout, number, table, lasts[number], parts[number], helds[number], out, parts[number + 1 :]
        )
    out = final_call(layout, last, table, lasts[last], parts[last], helds[last], out)
    return out[None, None]


def solution(mesh):
    in_specs = (
        P("row", "col", None, None, None),
        P("row", "col", None, None, None),
        P(),
        P(),
        P(),
        P(),
        P(),
        P(),
    )
    out_specs = P("row", "col", None, None, None)
    return jax.shard_map(
        on_device, mesh=mesh, in_specs=in_specs, out_specs=out_specs, check_vma=False
    )
```

time: 159 us -> 150 us (0.943)
  local copies, waits for them, and re-layouts: 22.4 us -> 9.26 us
  waiting for transfers between devices: 77.7 us -> 83.8 us
  starting transfers between devices: 18.7 us -> 21.6 us
  Pallas kernels: 34.9 us -> 32.1 us
    unnamed x24 -> x10, local copies, waits for them, and re-layouts: 15.7 us -> 1.23 us
    ppermute x10 -> x11, waiting for transfers between devices: 0.03 us -> 13 us  [the longest x3 11.8 us: line_of_four(): lax.ppermute(after(piece, mid_out) if place else piece, 'col', out)]
    ppermute x1, waiting for transfers between devices: 34.4 us -> 29.4 us  [line_of_four(): near = lax.ppermute(left, 'col', [(0, 1), (1, 0), (2, 3), (3, 2)])]
    pallas_call x4, Pallas kernels: 34.9 us -> 32.1 us  [the longest x1 17.3 us: main_call(): pl.pallas_call(functools.partial(main_kernel, routes, takers, pieces, lay...]
    ppermute x1, waiting for transfers between devices: 43.2 us -> 41.4 us  [line_of_four(): mid_out = lax.ppermute(mid_in, 'col', out)]
    slice x0 -> x1, local copies, waits for them, and re-layouts: none -> 1.68 us  [passed_on(): two[half:]]
    ppermute x10 -> x11, starting transfers between devices: 12.4 us -> 13.7 us  [the longest x3 6.31 us: send(): return lax.ppermute(value, 'row', pairs)]
  transfers between devices with their start and end apart: 13 -> 14, of which waited for: 2 -> 5; matrix products, arithmetic and copies ran while one was open for 6% -> 7% of each run, Pallas kernels for 20% -> 20%
where the time goes in v2:
time: 150 us; the launch traced here: 149 us
  waiting for transfers between devices  83.8 us (56%)
  Pallas kernels  32.1 us (21%)
  starting transfers between devices  21.6 us (14%)
  local copies, waits for them, and re-layouts  9.26 us (6%)
  other arithmetic  2.14 us (1%)
    ppermute x1, waiting for transfers between devices, line_of_four(): mid_out = lax.ppermute(mid_in, 'col', out)  41.4 us
    ppermute x1, waiting for transfers between devices, line_of_four(): near = lax.ppermute(left, 'col', [(0, 1), (1, 0), (2, 3), (3, 2)])  29.4 us
    pallas_call x1, Pallas kernels, main_call(): pl.pallas_call(functools.partial(main_kernel, routes, takers, pieces, lay...  17.3 us
    pallas_call x2, Pallas kernels, piece_call(): pl.pallas_call(functools.partial(piece_kernel, len(lasts), later, layout,...  12.4 us
    ppermute x3, waiting for transfers between devices, line_of_four(): lax.ppermute(after(piece, mid_out) if place else piece, 'col', out)  11.8 us
    ppermute x3, starting transfers between devices, send(): return lax.ppermute(value, 'row', pairs)  6.31 us
    ppermute x1, starting transfers between devices, line_of_four(): near = lax.ppermute(left, 'col', [(0, 1), (1, 0), (2, 3), (3, 2)])  4.53 us
    ppermute x3, starting transfers between devices, line_of_four(): lax.ppermute(after(piece, mid_out) if place else piece, 'col', out)  3.85 us
  transfers between devices with their start and end apart: 14, of which 5 were waited for; matrix products, arithmetic and copies ran while one was open for 7% of the time, Pallas kernels for 20%

profile of v2, /device:TPU:0, one launch (start us, length us, event | category | flops | bytes accessed | tf_op | source)
XLA Modules:
  0.0 149.3 jit_solution(10758571667537371406)
XLA Ops:
  0.0 2.0 %collective-permute-start.1 = (bf16[16,256,256]{2,1,0:T(8,128)(2,1)}, bf16[16,256,256]{2,1,0:T(8,128)(2,1)}, u32[]{:S(2)}, u32[]{:S(2)}) collective-permute-start(bf16[16,256,256]{2,1,0:T(8,128)(2,1)} %bitcast.33), channel_id=1, source_target_pairs={{1,2},{2,1},{5,6},{6,5},{9,10},{10,9},{13,14},{14,13},{17,18},{18,... | collective-permute-start | bytes 6291464 | tf_op jit(solution)/shard_map/ppermute | solution.py:361
  2.0 4.5 %collective-permute-start = (bf16[16,256,256]{2,1,0:T(8,128)(2,1)}, bf16[16,256,256]{2,1,0:T(8,128)(2,1)S(1)}, u32[]{:S(2)}, u32[]{:S(2)}) collective-permute-start(bf16[16,256,256]{2,1,0:T(8,128)(2,1)} %bitcast.34), channel_id=1, source_target_pairs={{0,1},{1,0},{2,3},{3,2},{4,5},{5,4},{6,7},{7,6},{8,9},{9,8},{10,11... | collective-permute-start | bytes 6291464 | tf_op jit(solution)/shard_map/ppermute | solution.py:360
  6.6 3.6 %collective-permute-start.7 = (bf16[16,256,256]{2,1,0:T(8,128)(2,1)}, bf16[16,256,256]{2,1,0:T(8,128)(2,1)}, u32[]{:S(2)}, u32[]{:S(2)}) collective-permute-start(bf16[16,256,256]{2,1,0:T(8,128)(2,1)} %bitcast.36), channel_id=1, source_target_pairs={{16,4},{24,12},{0,20},{8,28},{17,5},{25,13},{1,21},{9,29},{18,6},{... | collective-permute-start | bytes 6291464 | tf_op jit(solution)/shard_map/ppermute | solution.py:392
  10.2 1.4 collective-permute-start.6
  11.6 1.3 collective-permute-start.5
  13.0 0.7 dynamic-slice_bitcast_fusion
  13.7 0.6 gather_fusion.2
  14.3 0.6 gather_fusion
  14.9 0.7 constant_dynamic-slice_fusion.1
  15.6 0.6 gather_fusion.3
  16.2 0.6 gather_fusion.1
  16.7 0.3 fusion
  17.0 0.1 fusion.8
  17.2 0.7 fusion.5
  17.9 0.3 select_reduce_fusion.1
  18.3 0.3 select_reduce_fusion
  18.7 0.1 copy.30
  18.8 0.1 slice.43
  19.0 0.1 slice.39
  19.1 0.1 copy.29
  19.3 0.2 select_reduce_fusion.2
  19.6 0.2 convert_reduce_fusion.2
  19.8 0.1 copy.27
  19.9 0.1 reshape.385
  20.0 0.1 copy.24
  20.1 0.1 add.123
  20.3 0.2 select_reduce_fusion.3
  20.5 1.3 collective-permute-start.3
  21.8 0.2 convert_reduce_fusion
  22.0 0.7 concatenate.37.table_ref
  22.7 29.4 %collective-permute-done.refs_1_ = bf16[16,256,256]{2,1,0:T(8,128)(2,1)S(1)} collective-permute-done((bf16[16,256,256]{2,1,0:T(8,128)(2,1)}, bf16[16,256,256]{2,1,0:T(8,128)(2,1)S(1)}, u32[]{:S(2)}, u32[]{:S(2)}) %collective-permute-start) | collective-permute-done | bytes 2097184 | tf_op jit(solution)/shard_map/ppermute | solution.py:360
  52.2 1.6 %collective-permute-start.10 = (bf16[8,256,256]{2,1,0:T(8,128)(2,1)S(1)}, bf16[8,256,256]{2,1,0:T(8,128)(2,1)}, u32[]{:S(2)}, u32[]{:S(2)}) collective-permute-start(bf16[8,256,256]{2,1,0:T(8,128)(2,1)S(1)} %slice.46), channel_id=1, source_target_pairs={{1,2},{2,1},{5,6},{6,5},{9,10},{10,9},{13,14},{14,13},{17,18},{18,... | collective-permute-start | bytes 3145736 | tf_op jit(solution)/shard_map/ppermute | solution.py:365
  53.9 1.1 collective-permute-done.6.refs_6_
  55.1 0.7 collective-permute-start.8
  55.8 1.7 %fusion.15 = (bf16[8,256,256]{2,1,0:T(8,128)(2,1)S(1)}, bf16[8,256,256]{2,1,0:T(8,128)(2,1)S(1)}) fusion(bf16[16,256,256]{2,1,0:T(8,128)(2,1)} %collective-permute-done.6.refs_6_), kind=kLoop, calls=%fused_computation.71 | loop fusion | bytes 4194304 | tf_op jit(solution)/shard_map/slice | solution.py:404
  57.5 0.5 collective-permute-start.12
  58.0 1.3 collective-permute-start.11
  59.3 41.4 %collective-permute-done.3.refs_3_ = bf16[16,256,256]{2,1,0:T(8,128)(2,1)} collective-permute-done((bf16[16,256,256]{2,1,0:T(8,128)(2,1)}, bf16[16,256,256]{2,1,0:T(8,128)(2,1)}, u32[]{:S(2)}, u32[]{:S(2)}) %collective-permute-start.3) | collective-permute-done | bytes 2097184 | tf_op jit(solution)/shard_map/ppermute | solution.py:362
  100.7 1.3 collective-permute-start.9
  102.0 0.7 collective-permute-start.2
  102.7 1.3 collective-permute-start.4
  104.1 17.3 %first_panels.1 = (bf16[64,256,256]{2,1,0:T(8,128)(2,1)}, f32[16,256,256]{2,1,0:T(8,128)}, f32[12,256,256]{2,1,0:T(8,128)}, f32[4,256,256]{2,1,0:T(8,128)}, bf16...) custom-call(s32[374]{0:T(512)} %concatenate.37.table_ref, ...), custom_call_target="tpu_custom_call" | custom-call | flops 1048576 | bytes 65536 | tf_op jit(solution)/shard_map/first_panels/pallas_call | solution.py:144
  121.4 1.8 %collective-permute-done.11.refs_1_ = bf16[8,256,256]{2,1,0:T(8,128)(2,1)} collective-permute-done((bf16[8,256,256]{2,1,0:T(8,128)(2,1)}, bf16[8,256,256]{2,1,0:T(8,128)(2,1)}, u32[]{:S(2)}, u32[]{:S(2)}) %collective-permute-start.11) | collective-permute-done | bytes 1048608 | tf_op jit(solution)/shard_map/ppermute | solution.py:369
  123.2 6.8 %last_panel_piece.2 = (bf16[64,256,256]{2,1,0:T(8,128)(2,1)}, f32[12,256,256]{2,1,0:T(8,128)}, f32[4,256,256]{2,1,0:T(8,128)}) custom-call(s32[374]{0:T(512)} %concatenate.37.table_ref, bf16[8,256,256]{2,1,0:T(8,128)(2,1)} %collective-permute-done.10.refs_0_, ...), custom_call_target="tpu_custom_call", output_to_operand_aliasing={{0}: (5, {}), {1}: (6, {}), {2}: (7, {})} | custom-call | flops 1048576 | bytes 65536 | tf_op jit(solution)/shard_map/last_panel_piece/pallas_call | solution.py:243
  130.0 10.0 %collective-permute-done.9.refs_1_ = bf16[6,256,256]{2,1,0:T(8,128)(2,1)} collective-permute-done((bf16[6,256,256]{2,1,0:T(8,128)(2,1)S(1)}, bf16[6,256,256]{2,1,0:T(8,128)(2,1)}, u32[]{:S(2)}, u32[]{:S(2)}) %collective-permute-start.9) | collective-permute-done | bytes 786464 | tf_op jit(solution)/shard_map/ppermute | solution.py:369
  140.0 5.6 %last_panel_piece.3 = (bf16[64,256,256]{2,1,0:T(8,128)(2,1)}, f32[4,256,256]{2,1,0:T(8,128)}) custom-call(s32[374]{0:T(512)} %concatenate.37.table_ref, bf16[6,256,256]{2,1,0:T(8,128)(2,1)} %copy-done.4, bf16[6,256,256]{2,1,0:T(8,128)(2,1)} %collective-permute-done.9.refs_1_, ...), custom_call_target="tpu_custom_call", output_to_operand_aliasing={{0}: (5, {}), {1}: (6, {})} | custom-call | flops 1048576 | bytes 65536 | tf_op jit(solution)/shard_map/last_panel_piece/pallas_call | solution.py:243
  145.7 1.2 copy-done
  146.9 2.4 %last_piece.1 = bf16[64,256,256]{2,1,0:T(8,128)(2,1)} custom-call(s32[374]{0:T(512)S(1)} %copy-done.2, bf16[2,256,256]{2,1,0:T(8,128)(2,1)S(1)} %collective-permute-done.2.refs_0_, bf16[2,256,256]{2,1,0:T(8,128)(2,1)S(1)} %collective-permute-done.4.refs_1_, f32[4,256,256]{2,1,0:T(8,128)S(1)} %copy-done, ...), custom_call_target="tpu_custom_call", output_to_operand_aliasing={{}: (5, {})} | custom-call | flops 1048576 | bytes 65536 | tf_op jit(solution)/shard_map/last_piece/pallas_call | solution.py:320
  (43 shorter events, 0.9 us)
Async XLA Ops:
  0.0 20.5 %collective-permute-start.1 = (bf16[16,256,256]{2,1,0:T(8,128)(2,1)}, bf16[16,256,256]{2,1,0:T(8,128)(2,1)}, u32[]{:S(2)}, u32[]{:S(2)}) collective-permute-start(bf16[16,256,256]{2,1,0:T(8,128)(2,1)} %bitcast.33), channel_id=1, source_target_pairs={{1,2},{2,1},{5,6},{6,5},{9,10},{10,9},{13,14},{14,13},{17,18},{18,... | collective-permute-start | bytes 6291464 | tf_op jit(solution)/shard_map/ppermute | solution.py:361
  2.0 50.1 %collective-permute-start = (bf16[16,256,256]{2,1,0:T(8,128)(2,1)}, bf16[16,256,256]{2,1,0:T(8,128)(2,1)S(1)}, u32[]{:S(2)}, u32[]{:S(2)}) collective-permute-start(bf16[16,256,256]{2,1,0:T(8,128)(2,1)} %bitcast.34), channel_id=1, source_target_pairs={{0,1},{1,0},{2,3},{3,2},{4,5},{5,4},{6,7},{7,6},{8,9},{9,8},{10,11... | collective-permute-start | bytes 6291464 | tf_op jit(solution)/shard_map/ppermute | solution.py:360
  6.6 47.3 %collective-permute-start.7 = (bf16[16,256,256]{2,1,0:T(8,128)(2,1)}, bf16[16,256,256]{2,1,0:T(8,128)(2,1)}, u32[]{:S(2)}, u32[]{:S(2)}) collective-permute-start(bf16[16,256,256]{2,1,0:T(8,128)(2,1)} %bitcast.36), channel_id=1, source_target_pairs={{16,4},{24,12},{0,20},{8,28},{17,5},{25,13},{1,21},{9,29},{18,6},{... | collective-permute-start | bytes 6291464 | tf_op jit(solution)/shard_map/ppermute | solution.py:392
  10.2 44.9 %collective-permute-start.6 = (bf16[16,256,256]{2,1,0:T(8,128)(2,1)}, bf16[16,256,256]{2,1,0:T(8,128)(2,1)}, u32[]{:S(2)}, u32[]{:S(2)}) collective-permute-start(bf16[16,256,256]{2,1,0:T(8,128)(2,1)} %bitcast.37), channel_id=1, source_target_pairs={{8,0},{12,4},{16,8},{20,12},{24,16},{28,20},{0,24},{4,28},{9,1},{1... | collective-permute-start | bytes 6291464 | tf_op jit(solution)/shard_map/ppermute | solution.py:392
  11.6 43.4 %collective-permute-start.5 = (bf16[16,256,256]{2,1,0:T(8,128)(2,1)}, bf16[16,256,256]{2,1,0:T(8,128)(2,1)}, u32[]{:S(2)}, u32[]{:S(2)}) collective-permute-start(bf16[16,256,256]{2,1,0:T(8,128)(2,1)} %bitcast.38), channel_id=1, source_target_pairs={{4,0},{12,8},{20,16},{28,24},{5,1},{13,9},{21,17},{29,25},{6,2},{1... | collective-permute-start | bytes 6291464 | tf_op jit(solution)/shard_map/ppermute | solution.py:392
  20.5 80.2 %collective-permute-start.3 = (bf16[16,256,256]{2,1,0:T(8,128)(2,1)}, bf16[16,256,256]{2,1,0:T(8,128)(2,1)}, u32[]{:S(2)}, u32[]{:S(2)}) collective-permute-start(bf16[16,256,256]{2,1,0:T(8,128)(2,1)} %collective-permute-done.1.refs_2_), channel_id=1, source_target_pairs={{2,3},{1,0},{6,7},{5,4},{10,11},{9,8},{14,15},{13,12},{18,19},{17,... | collective-permute-start | bytes 6291464 | tf_op jit(solution)/shard_map/ppermute | solution.py:362
  52.1 49.9 %copy-start.3 = (bf16[16,256,256]{2,1,0:T(8,128)(2,1)}, bf16[16,256,256]{2,1,0:T(8,128)(2,1)S(1)}, u32[]{:S(2)}) copy-start(bf16[16,256,256]{2,1,0:T(8,128)(2,1)S(1)} %collective-permute-done.refs_1_) | copy-start | bytes 6291460
  52.2 5.8 %collective-permute-start.10 = (bf16[8,256,256]{2,1,0:T(8,128)(2,1)S(1)}, bf16[8,256,256]{2,1,0:T(8,128)(2,1)}, u32[]{:S(2)}, u32[]{:S(2)}) collective-permute-start(bf16[8,256,256]{2,1,0:T(8,128)(2,1)S(1)} %slice.46), channel_id=1, source_target_pairs={{1,2},{2,1},{5,6},{6,5},{9,10},{10,9},{13,14},{14,13},{17,18},{18,... | collective-permute-start | bytes 3145736 | tf_op jit(solution)/shard_map/ppermute | solution.py:365
  55.1 4.3 %collective-permute-start.8 = (bf16[6,256,256]{2,1,0:T(8,128)(2,1)S(1)}, bf16[6,256,256]{2,1,0:T(8,128)(2,1)S(1)}, u32[]{:S(2)}, u32[]{:S(2)}) collective-permute-start(bf16[6,256,256]{2,1,0:T(8,128)(2,1)S(1)} %slice.45), channel_id=1, source_target_pairs={{1,2},{2,1},{5,6},{6,5},{9,10},{10,9},{13,14},{14,13},{17,18},{18,... | collective-permute-start | bytes 2359304 | tf_op jit(solution)/shard_map/ppermute | solution.py:365
  57.4 46.6 %collective-permute-start.13 = (bf16[8,256,256]{2,1,0:T(8,128)(2,1)S(1)}, bf16[8,256,256]{2,1,0:T(8,128)(2,1)}, u32[]{:S(2)}, u32[]{:S(2)}) collective-permute-start(bf16[8,256,256]{2,1,0:T(8,128)(2,1)S(1)} %get-tuple-element.48), channel_id=1, source_target_pairs={{0,4},{4,0},{8,12},{12,8},{16,20},{20,16},{24,28},{28,24},{1,5},{5... | collective-permute-start | bytes 3145736 | tf_op jit(solution)/shard_map/ppermute | solution.py:404
  57.5 46.5 %collective-permute-start.12 = (bf16[8,256,256]{2,1,0:T(8,128)(2,1)S(1)}, bf16[8,256,256]{2,1,0:T(8,128)(2,1)}, u32[]{:S(2)}, u32[]{:S(2)}) collective-permute-start(bf16[8,256,256]{2,1,0:T(8,128)(2,1)S(1)} %get-tuple-element.49), channel_id=1, source_target_pairs={{0,4},{4,0},{8,12},{12,8},{16,20},{20,16},{24,28},{28,24},{1,5},{5... | collective-permute-start | bytes 3145736 | tf_op jit(solution)/shard_map/ppermute | solution.py:404
  58.0 65.2 %collective-permute-start.11 = (bf16[8,256,256]{2,1,0:T(8,128)(2,1)}, bf16[8,256,256]{2,1,0:T(8,128)(2,1)}, u32[]{:S(2)}, u32[]{:S(2)}) collective-permute-start(bf16[8,256,256]{2,1,0:T(8,128)(2,1)} %collective-permute-done.10.refs_0_), channel_id=1, source_target_pairs={{2,3},{1,0},{6,7},{5,4},{10,11},{9,8},{14,15},{13,12},{18,19},{17,... | collective-permute-start | bytes 3145736 | tf_op jit(solution)/shard_map/ppermute | solution.py:369
  59.3 62.1 %copy-start.4 = (bf16[6,256,256]{2,1,0:T(8,128)(2,1)}, bf16[6,256,256]{2,1,0:T(8,128)(2,1)S(1)}, u32[]{:S(2)}) copy-start(bf16[6,256,256]{2,1,0:T(8,128)(2,1)S(1)} %collective-permute-done.8.refs_0_) | copy-start | bytes 2359300
  100.7 39.3 %collective-permute-start.9 = (bf16[6,256,256]{2,1,0:T(8,128)(2,1)S(1)}, bf16[6,256,256]{2,1,0:T(8,128)(2,1)}, u32[]{:S(2)}, u32[]{:S(2)}) collective-permute-start(bf16[6,256,256]{2,1,0:T(8,128)(2,1)S(1)} %collective-permute-done.8.refs_0_), channel_id=1, source_target_pairs={{2,3},{1,0},{6,7},{5,4},{10,11},{9,8},{14,15},{13,12},{18,19},{17,... | collective-permute-start | bytes 2359304 | tf_op jit(solution)/shard_map/ppermute | solution.py:369
  102.0 0.7 collective-permute-start.2
  102.7 42.9 %collective-permute-start.4 = (bf16[2,256,256]{2,1,0:T(8,128)(2,1)S(1)}, bf16[2,256,256]{2,1,0:T(8,128)(2,1)S(1)}, u32[]{:S(2)}, u32[]{:S(2)}) collective-permute-start(bf16[2,256,256]{2,1,0:T(8,128)(2,1)S(1)} %collective-permute-done.2.refs_0_), channel_id=1, source_target_pairs={{2,3},{1,0},{6,7},{5,4},{10,11},{9,8},{14,15},{13,12},{18,19},{17,... | collective-permute-start | bytes 786440 | tf_op jit(solution)/shard_map/ppermute | solution.py:369
  140.0 5.6 %copy-start.1 = (bf16[4,256,256]{2,1,0:T(8,128)(2,1)S(1)}, bf16[4,256,256]{2,1,0:T(8,128)(2,1)}, u32[]{:S(2)}) copy-start(bf16[4,256,256]{2,1,0:T(8,128)(2,1)} %get-tuple-element.35.refs_3_) | copy-start | bytes 1572868
  140.0 5.6 %copy-start.2 = (s32[374]{0:T(512)S(1)}, s32[374]{0:T(512)}, u32[]{:S(2)}) copy-start(s32[374]{0:T(512)} %concatenate.37.table_ref) | copy-start | bytes 4492
  145.7 1.2 copy-start

commit v3 on v2

--- a/solution.py
+++ b/solution.py
@@ -9,6 +9,7 @@
 
 STEPS = 4
 VMEM_BYTES = 60 * 2**20
+PIECE_VMEM = 40 * 2**20
 FINAL_VMEM = 16 * 2**20
 UNROLL = 4
 SMALL = pl.CostEstimate(flops=2**20, bytes_accessed=2**16, transcendentals=0)
@@ -168,52 +169,40 @@
     return result[0], list(result[1 : 1 + len(pieces)]), list(result[1 + len(pieces) :])
 
 
-def piece_kernel(choices, later, layout, number, table_ref, *refs):
+def piece_kernel(choices, later, fresh, layout, number, table_ref, *refs):
     def entry(name, pair):
         return table_ref[layout[name, number] + pair]
 
     lasts, refs = refs[:choices], refs[choices:]
-    part_hbm, held_hbm, refs = refs[0], refs[1], refs[3 + len(later) :]
+    part_hbm, held_hbm, before, refs = refs[0], refs[1], refs[3 : 3 + len(later)], refs[3 + len(later) :]
     out_ref, later_refs, refs = refs[0], refs[1 : 1 + len(later)], refs[1 + len(later) :]
-    left, part, held, staged, left_sem, held_sem, part_sem, out_sem, later_sem = refs
+    left, part, held, products, staged, in_sem, out_sem, later_sem = refs
     pairs = part.shape[0]
 
-    def left_copy(block, place):
-        return pltpu.make_async_copy(
-            lasts[place].at[block], left.at[block], left_sem.at[block]
-        )
-
-    def held_copy(pair):
-        return pltpu.make_async_copy(held_hbm.at[pair], held.at[pair], held_sem.at[pair])
-
-    def part_copy(pair):
-        return pltpu.make_async_copy(part_hbm.at[pair], part.at[pair], part_sem.at[pair])
+    left_copies = [pltpu.make_async_copy(last, left, in_sem.at[0]) for last in lasts]
+    held_copy = pltpu.make_async_copy(held_hbm, held, in_sem.at[1])
+    part_copy = pltpu.make_async_copy(part_hbm, part, in_sem.at[2])
 
     def out_copy(pair):
         return pltpu.make_async_copy(
             staged.at[pair], out_ref.at[entry("here", pair)], out_sem.at[pair]
         )
 
-    for block in range(pairs // 2):
-        for place in range(choices):
-            pl.when(table_ref[layout["flags"]] == place)(
-                lambda block=block, place=place: left_copy(block, place).start()
-            )
-        for pair in (2 * block, 2 * block + 1):
-            held_copy(pair).start()
-            part_copy(pair).start()
-
-    for pair in range(pairs):
-        if pair % 2 == 0:
-            left_copy(pair // 2, 0).wait()
-        held_copy(pair).wait()
-        part_copy(pair).wait()
-        lead = entry("lead", pair)
-        total = part[lead] + jnp.dot(
+    held_copy.start()
+    part_copy.start()
+    for place, copy in enumerate(left_copies):
+        pl.when(table_ref[layout["flags"]] == place)(copy.start)
+    left_copies[0].wait()
+    held_copy.wait()
+    for pair in range(pairs):
+        products[pair] = jnp.dot(
             left[pair // 2], held[pair], preferred_element_type=jnp.float32
         )
-        part[lead] = total
-        staged[pair] = total.astype(staged.dtype)
+    part_copy.wait()
+    for pair in range(pairs):
+        part[entry("lead", pair)] += products[pair]
+    for pair in range(pairs):
+        staged[pair] = part[entry("lead", pair)].astype(staged.dtype)
         pl.when(entry("final", pair) == 1)(lambda pair=pair: out_copy(pair).start())
 
     tails = []
@@ -226,40 +215,52 @@
             part.at[entry("link", pair)], later_refs[piece].at[place], later_sem.at[pair]
         )
 
-    for pair in range(len(tails)):
-        pl.when(entry("link", pair) >= 0)(lambda pair=pair: later_copy(pair).start())
+    def kept_copy(pair):
+        piece, place = tails[pair]
+        return pltpu.make_async_copy(
+            before[piece].at[place], later_refs[piece].at[place], later_sem.at[pair]
+        )
+
+    def each_later(act):
+        for pair in range(len(tails)):
+            link = entry("link", pair)
+            pl.when(link >= 0)(lambda pair=pair: act(later_copy(pair)))
+            if fresh:
+                pl.when(link < 0)(lambda pair=pair: act(kept_copy(pair)))
+
+    each_later(lambda copy: copy.start())
     for pair in range(pairs):
         pl.when(entry("final", pair) == 1)(lambda pair=pair: out_copy(pair).wait())
-    for pair in range(len(tails)):
-        pl.when(entry("link", pair) >= 0)(lambda pair=pair: later_copy(pair).wait())
-
-
-def piece_call(layout, number, table, lasts, part, held, out, later_parts):
+    each_later(lambda copy: copy.wait())
+
+
+def piece_call(layout, number, table, lasts, part, held, out, later_parts, fresh):
     smem = pl.BlockSpec(memory_space=pltpu.SMEM)
     hbm = pl.BlockSpec(memory_space=pl.ANY)
     pairs, width = held.shape[0], held.shape[1]
     later = [value.shape[0] // 2 for value in later_parts]
     first_alias = 1 + len(lasts) + 2
     result = pl.pallas_call(
-        functools.partial(piece_kernel, len(lasts), later, layout, number),
+        functools.partial(piece_kernel, len(lasts), later, fresh, layout, number),
         out_shape=tuple(
             jax.ShapeDtypeStruct(value.shape, value.dtype) for value in (out, *later_parts)
         ),
         in_specs=[smem] + [hbm] * (len(lasts) + 3 + len(later)),
         out_specs=(hbm,) * (1 + len(later)),
-        input_output_aliases={first_alias + place: place for place in range(1 + len(later))},
+        input_output_aliases={
+            first_alias + place: place for place in range(1 if fresh else 1 + len(later))
+        },
         scratch_shapes=[
             pltpu.VMEM(lasts[0].shape, lasts[0].dtype),
             pltpu.VMEM(part.shape, part.dtype),
             pltpu.VMEM(held.shape, held.dtype),
+            pltpu.VMEM(part.shape, part.dtype),
             pltpu.VMEM(held.shape, held.dtype),
-            pltpu.SemaphoreType.DMA((pairs // 2,)),
-            pltpu.SemaphoreType.DMA((pairs,)),
-            pltpu.SemaphoreType.DMA((pairs,)),
+            pltpu.SemaphoreType.DMA((3,)),
             pltpu.SemaphoreType.DMA((pairs,)),
             pltpu.SemaphoreType.DMA((max(1, 2 * sum(later)),)),
         ],
-        compiler_params=pltpu.CompilerParams(vmem_limit_bytes=VMEM_BYTES),
+        compiler_params=pltpu.CompilerParams(vmem_limit_bytes=PIECE_VMEM if fresh else VMEM_BYTES),
         cost_estimate=SMALL,
         name="last_panel_piece",
     )(table, *lasts, part, held, out, *later_parts)
@@ -268,14 +269,10 @@
 
 def final_kernel(choices, layout, number, table_ref, *refs):
     lasts, refs = refs[:choices], refs[choices:]
-    part_hbm, held, _, out_ref, part, totals, staged, part_sem, out_sem = refs
+    part_hbm, held, _, out_ref, part, products, staged, part_sem, out_sem = refs
     pairs = part.shape[0]
-    part_copies = [
-        pltpu.make_async_copy(part_hbm.at[pair], part.at[pair], part_sem.at[pair])
-        for pair in range(pairs)
-    ]
-    for copy in part_copies:
-        copy.start()
+    part_copy = pltpu.make_async_copy(part_hbm, part, part_sem)
+    part_copy.start()
 
     def entry(name, pair):
         return table_ref[layout[name, number] + pair]
@@ -285,28 +282,19 @@
             staged.at[pair], out_ref.at[entry("here", pair)], out_sem.at[pair]
         )
 
+    flag = table_ref[layout["flags"]]
     for block in range(pairs // 2):
         left = lasts[0][block]
         for place in range(1, choices):
-            left = jnp.where(table_ref[layout["flags"]] == place, lasts[place][block], left)
+            left = jnp.where(flag == place, lasts[place][block], left)
         for pair in (2 * block, 2 * block + 1):
-            lead = entry("lead", pair)
-            product = jnp.dot(left, held[pair], preferred_element_type=jnp.float32)
-            part_copies[pair].wait()
-
-            @pl.when(lead == pair)
-            def _():
-                totals[pair] = part[pair] + product
-
-            @pl.when(lead != pair)
-            def _():
-                totals[lead] += product
-
-            @pl.when(entry("final", pair) == 1)
-            def _():
-                staged[pair] = totals[lead].astype(staged.dtype)
-                out_copy(pair).start()
-
+            products[pair] = jnp.dot(left, held[pair], preferred_element_type=jnp.float32)
+    part_copy.wait()
+    for pair in range(pairs):
+        part[entry("lead", pair)] += products[pair]
+    for pair in range(pairs):
+        staged[pair] = part[entry("lead", pair)].astype(staged.dtype)
+        pl.when(entry("final", pair) == 1)(lambda pair=pair: out_copy(pair).start())
     for pair in range(pairs):
         pl.when(entry("final", pair) == 1)(lambda pair=pair: out_copy(pair).wait())
 
@@ -327,7 +315,7 @@
             pltpu.VMEM(part.shape, part.dtype),
             pltpu.VMEM(part.shape, part.dtype),
             pltpu.VMEM(held.shape, held.dtype),
-            pltpu.SemaphoreType.DMA((pairs,)),
+            pltpu.SemaphoreType.DMA,
             pltpu.SemaphoreType.DMA((pairs,)),
         ],
         compiler_params=pltpu.CompilerParams(vmem_limit_bytes=FINAL_VMEM),
@@ -465,8 +453,8 @@
     left, right = a_panels[0, 0], b_panels[0, 0]
     own_rows, own_cols = c_rows[row_id, col_id], c_cols[row_id, col_id]
     on_line = lax.axis_size("col") == STEPS
-    eighth = left.shape[0] // 8
-    far_sizes = (left.shape[0] - 4 * eighth, 3 * eighth, eighth)
+    blocks = left.shape[0]
+    far_sizes = (blocks // 2, blocks - blocks // 2 - 3 * blocks // 16, 3 * blocks // 16)
     columns = (line_columns if on_line else ring_columns)(col_id)
     picks, slots = pair_tables(columns, a_rows, a_inner, b_inner, b_cols, own_rows, own_cols)
     at_end = on_line & ((col_id == 0) | (col_id == 3))
@@ -490,7 +478,7 @@
     last = len(far_sizes) - 1
     for number in range(last):
         out, parts[number + 1 :] = piece_call(
-            layout, number, table, lasts[number], parts[number], helds[number], out, parts[number + 1 :]
+            layout, number, table, lasts[number], parts[number], helds[number], out, parts[number + 1 :], number == last - 1
         )
     out = final_call(layout, last, table, lasts[last], parts[last], helds[last], out)
     return out[None, None]

time: 150 us -> 146 us (0.973)
  waiting for transfers between devices: 83.8 us -> 80.4 us
  local copies, waits for them, and re-layouts: 9.26 us -> 12.2 us
  Pallas kernels: 32.1 us -> 29.2 us
    unnamed x10 -> x14, local copies, waits for them, and re-layouts: 1.23 us -> 4.13 us
    ppermute x3, waiting for transfers between devices: 11.8 us -> 9.16 us  [line_of_four(): lax.ppermute(after(piece, mid_out) if place else piece, 'col', out)]
    pallas_call x2, Pallas kernels: 12.4 us -> 9.81 us  [piece_call(): pl.pallas_call(functools.partial(piece_kernel, len(lasts), later, fresh,...]
  transfers between devices with their start and end apart: 14 -> 14, of which waited for: 5 -> 6; matrix products, arithmetic and copies ran while one was open for 7% -> 7% of each run, Pallas kernels for 20% -> 19%
where the time goes in v3:
time: 146 us
  waiting for transfers between devices  80.4 us (55%)
  Pallas kernels  29.2 us (20%)
  starting transfers between devices  21.7 us (15%)
  local copies, waits for them, and re-layouts  12.2 us (8%)
  other arithmetic  2.12 us (1%)
    ppermute x1, waiting for transfers between devices, line_of_four(): mid_out = lax.ppermute(mid_in, 'col', out)  40.7 us
    ppermute x1, waiting for transfers between devices, line_of_four(): near = lax.ppermute(left, 'col', [(0, 1), (1, 0), (2, 3), (3, 2)])  29.4 us
    pallas_call x1, Pallas kernels, main_call(): pl.pallas_call(functools.partial(main_kernel, routes, takers, pieces, lay...  17.3 us
    pallas_call x2, Pallas kernels, piece_call(): pl.pallas_call(functools.partial(piece_kernel, len(lasts), later, fresh,...  9.81 us
    ppermute x3, waiting for transfers between devices, line_of_four(): lax.ppermute(after(piece, mid_out) if place else piece, 'col', out)  9.16 us
    ppermute x3, starting transfers between devices, send(): return lax.ppermute(value, 'row', pairs)  6.32 us
    ppermute x1, starting transfers between devices, line_of_four(): near = lax.ppermute(left, 'col', [(0, 1), (1, 0), (2, 3), (3, 2)])  4.52 us
    unnamed x14, local copies, waits for them, and re-layouts  4.13 us
  transfers between devices with their start and end apart: 14, of which 6 were waited for; matrix products, arithmetic and copies ran while one was open for 7% of the time, Pallas kernels for 19%

profile of v3, /device:TPU:0, one launch (start us, length us, event | category | flops | bytes accessed | tf_op | source)
XLA Modules:
  0.0 145.9 jit_solution(12859724090304956788)
XLA Ops:
  0.0 2.0 %collective-permute-start.1 = (bf16[16,256,256]{2,1,0:T(8,128)(2,1)}, bf16[16,256,256]{2,1,0:T(8,128)(2,1)}, u32[]{:S(2)}, u32[]{:S(2)}) collective-permute-start(bf16[16,256,256]{2,1,0:T(8,128)(2,1)} %bitcast.33), channel_id=1, source_target_pairs={{1,2},{2,1},{5,6},{6,5},{9,10},{10,9},{13,14},{14,13},{17,18},{18,... | collective-permute-start | bytes 6291464 | tf_op jit(solution)/shard_map/ppermute | solution.py:349
  2.0 4.5 %collective-permute-start = (bf16[16,256,256]{2,1,0:T(8,128)(2,1)}, bf16[16,256,256]{2,1,0:T(8,128)(2,1)S(1)}, u32[]{:S(2)}, u32[]{:S(2)}) collective-permute-start(bf16[16,256,256]{2,1,0:T(8,128)(2,1)} %bitcast.34), channel_id=1, source_target_pairs={{0,1},{1,0},{2,3},{3,2},{4,5},{5,4},{6,7},{7,6},{8,9},{9,8},{10,11... | collective-permute-start | bytes 6291464 | tf_op jit(solution)/shard_map/ppermute | solution.py:348
  6.6 3.6 %collective-permute-start.7 = (bf16[16,256,256]{2,1,0:T(8,128)(2,1)}, bf16[16,256,256]{2,1,0:T(8,128)(2,1)}, u32[]{:S(2)}, u32[]{:S(2)}) collective-permute-start(bf16[16,256,256]{2,1,0:T(8,128)(2,1)} %bitcast.36), channel_id=1, source_target_pairs={{16,4},{24,12},{0,20},{8,28},{17,5},{25,13},{1,21},{9,29},{18,6},{... | collective-permute-start | bytes 6291464 | tf_op jit(solution)/shard_map/ppermute | solution.py:380
  10.2 1.4 collective-permute-start.6
  11.6 1.3 collective-permute-start.5
  13.1 0.7 dynamic-slice_bitcast_fusion
  13.8 0.6 gather_fusion.2
  14.3 0.6 gather_fusion
  14.9 0.7 constant_dynamic-slice_fusion.1
  15.6 0.6 gather_fusion.3
  16.2 0.6 gather_fusion.1
  16.7 0.3 fusion
  17.2 0.3 select_reduce_fusion.1
  17.5 0.7 fusion.5
  18.3 0.3 select_reduce_fusion
  18.7 0.1 copy.26
  18.8 0.1 copy.29
  19.2 0.1 copy.28
  19.4 0.1 reshape.385
  19.5 0.1 copy.23
  19.6 0.1 add.123
  19.8 0.2 convert_reduce_fusion.2
  20.0 0.2 select_reduce_fusion.3
  20.2 0.2 select_reduce_fusion.2
  20.5 0.2 convert_reduce_fusion
  20.7 1.3 collective-permute-start.3
  22.0 0.7 concatenate.37.table_ref
  22.7 29.4 %collective-permute-done.refs_1_ = bf16[16,256,256]{2,1,0:T(8,128)(2,1)S(1)} collective-permute-done((bf16[16,256,256]{2,1,0:T(8,128)(2,1)}, bf16[16,256,256]{2,1,0:T(8,128)(2,1)S(1)}, u32[]{:S(2)}, u32[]{:S(2)}) %collective-permute-start) | collective-permute-done | bytes 2097184 | tf_op jit(solution)/shard_map/ppermute | solution.py:348
  52.2 1.7 %collective-permute-start.10 = (bf16[8,256,256]{2,1,0:T(8,128)(2,1)S(1)}, bf16[8,256,256]{2,1,0:T(8,128)(2,1)}, u32[]{:S(2)}, u32[]{:S(2)}) collective-permute-start(bf16[8,256,256]{2,1,0:T(8,128)(2,1)S(1)} %slice.46), channel_id=1, source_target_pairs={{1,2},{2,1},{5,6},{6,5},{9,10},{10,9},{13,14},{14,13},{17,18},{18,... | collective-permute-start | bytes 3145736 | tf_op jit(solution)/shard_map/ppermute | solution.py:353
  54.0 1.1 collective-permute-done.6.refs_6_
  55.1 0.7 collective-permute-start.8
  55.8 1.7 %fusion.15 = (bf16[8,256,256]{2,1,0:T(8,128)(2,1)S(1)}, bf16[8,256,256]{2,1,0:T(8,128)(2,1)S(1)}) fusion(bf16[16,256,256]{2,1,0:T(8,128)(2,1)} %collective-permute-done.6.refs_6_), kind=kLoop, calls=%fused_computation.71 | loop fusion | bytes 4194304 | tf_op jit(solution)/shard_map/slice | solution.py:392
  57.5 0.5 collective-permute-start.12
  58.0 1.3 collective-permute-start.11
  59.4 0.7 collective-permute-start.2
  60.1 40.7 %collective-permute-done.3.refs_3_ = bf16[16,256,256]{2,1,0:T(8,128)(2,1)} collective-permute-done((bf16[16,256,256]{2,1,0:T(8,128)(2,1)}, bf16[16,256,256]{2,1,0:T(8,128)(2,1)}, u32[]{:S(2)}, u32[]{:S(2)}) %collective-permute-start.3) | collective-permute-done | bytes 2097184 | tf_op jit(solution)/shard_map/ppermute | solution.py:350
  100.7 1.3 collective-permute-start.9
  102.0 1.3 collective-permute-start.4
  103.4 1.0 copy-done.6
  104.3 17.3 %first_panels.1 = (bf16[64,256,256]{2,1,0:T(8,128)(2,1)}, f32[16,256,256]{2,1,0:T(8,128)}, f32[10,256,256]{2,1,0:T(8,128)}, f32[6,256,256]{2,1,0:T(8,128)}, bf16...) custom-call(s32[376]{0:T(512)} %concatenate.37.table_ref, ...), custom_call_target="tpu_custom_call" | custom-call | flops 1048576 | bytes 65536 | tf_op jit(solution)/shard_map/first_panels/pallas_call | solution.py:145
  121.6 1.6 %collective-permute-done.11.refs_1_ = bf16[8,256,256]{2,1,0:T(8,128)(2,1)} collective-permute-done((bf16[8,256,256]{2,1,0:T(8,128)(2,1)}, bf16[8,256,256]{2,1,0:T(8,128)(2,1)}, u32[]{:S(2)}, u32[]{:S(2)}) %collective-permute-start.11) | collective-permute-done | bytes 1048608 | tf_op jit(solution)/shard_map/ppermute | solution.py:357
  123.2 6.8 %last_panel_piece.2 = (bf16[64,256,256]{2,1,0:T(8,128)(2,1)}, f32[10,256,256]{2,1,0:T(8,128)}, f32[6,256,256]{2,1,0:T(8,128)}) custom-call(s32[376]{0:T(512)} %concatenate.37.table_ref, bf16[8,256,256]{2,1,0:T(8,128)(2,1)} %collective-permute-done.10.refs_0_, ...), custom_call_target="tpu_custom_call", output_to_operand_aliasing={{0}: (5, {}), {1}: (6, {}), {2}: (7, {})} | custom-call | flops 1048576 | bytes 65536 | tf_op jit(solution)/shard_map/last_panel_piece/pallas_call | solution.py:243
  130.0 7.1 %collective-permute-done.9.refs_1_ = bf16[5,256,256]{2,1,0:T(8,128)(2,1)S(1)} collective-permute-done((bf16[5,256,256]{2,1,0:T(8,128)(2,1)S(1)}, bf16[5,256,256]{2,1,0:T(8,128)(2,1)S(1)}, u32[]{:S(2)}, u32[]{:S(2)}) %collective-permute-start.9) | collective-permute-done | bytes 655392 | tf_op jit(solution)/shard_map/ppermute | solution.py:357
  137.1 1.7 %copy-done = f32[10,256,256]{2,1,0:T(8,128)S(1)} copy-done((f32[10,256,256]{2,1,0:T(8,128)S(1)}, f32[10,256,256]{2,1,0:T(8,128)}, u32[]{:S(2)}) %copy-start) | copy-done | bytes 2621464
  138.9 1.4 copy-done.1
  140.3 3.0 %last_panel_piece.3 = (bf16[64,256,256]{2,1,0:T(8,128)(2,1)}, f32[6,256,256]{2,1,0:T(8,128)S(1)}) custom-call(s32[376]{0:T(512)S(1)} %copy-done.4, bf16[5,256,256]{2,1,0:T(8,128)(2,1)S(1)} %collective-permute-done.8.refs_0_, bf16[5,256,256]{2,1,0:T(8,128)(2,1)S(1)} %collective-permute-done.9.refs_1_, ...), custom_call_target="tpu_custom_call", output_to_operand_aliasing={{0}: (5, {})} | custom-call | flops 1048576 | bytes 65536 | tf_op jit(solution)/shard_map/last_panel_piece/pallas_call | solution.py:243
  143.3 0.5 collective-permute-done.4.refs_1_
  143.8 2.1 %last_piece.1 = bf16[64,256,256]{2,1,0:T(8,128)(2,1)} custom-call(s32[376]{0:T(512)S(1)} %copy-done.4, bf16[3,256,256]{2,1,0:T(8,128)(2,1)S(1)} %collective-permute-done.2.refs_0_, bf16[3,256,256]{2,1,0:T(8,128)(2,1)S(1)} %collective-permute-done.4.refs_1_, f32[6,256,256]{2,1,0:T(8,128)S(1)} %get-tuple-element.34.refs_2_, ...), custom_call_target="tpu_custom_call", output_to_operand_aliasing={{}: (5, {})} | custom-call | flops 1048576 | bytes 65536 | tf_op jit(solution)/shard_map/last_piece/pallas_call | solution.py:308
  (47 shorter events, 1.2 us)
Async XLA Ops:
  0.0 20.7 %collective-permute-start.1 = (bf16[16,256,256]{2,1,0:T(8,128)(2,1)}, bf16[16,256,256]{2,1,0:T(8,128)(2,1)}, u32[]{:S(2)}, u32[]{:S(2)}) collective-permute-start(bf16[16,256,256]{2,1,0:T(8,128)(2,1)} %bitcast.33), channel_id=1, source_target_pairs={{1,2},{2,1},{5,6},{6,5},{9,10},{10,9},{13,14},{14,13},{17,18},{18,... | collective-permute-start | bytes 6291464 | tf_op jit(solution)/shard_map/ppermute | solution.py:349
  2.0 50.1 %collective-permute-start = (bf16[16,256,256]{2,1,0:T(8,128)(2,1)}, bf16[16,256,256]{2,1,0:T(8,128)(2,1)S(1)}, u32[]{:S(2)}, u32[]{:S(2)}) collective-permute-start(bf16[16,256,256]{2,1,0:T(8,128)(2,1)} %bitcast.34), channel_id=1, source_target_pairs={{0,1},{1,0},{2,3},{3,2},{4,5},{5,4},{6,7},{7,6},{8,9},{9,8},{10,11... | collective-permute-start | bytes 6291464 | tf_op jit(solution)/shard_map/ppermute | solution.py:348
  6.6 47.4 %collective-permute-start.7 = (bf16[16,256,256]{2,1,0:T(8,128)(2,1)}, bf16[16,256,256]{2,1,0:T(8,128)(2,1)}, u32[]{:S(2)}, u32[]{:S(2)}) collective-permute-start(bf16[16,256,256]{2,1,0:T(8,128)(2,1)} %bitcast.36), channel_id=1, source_target_pairs={{16,4},{24,12},{0,20},{8,28},{17,5},{25,13},{1,21},{9,29},{18,6},{... | collective-permute-start | bytes 6291464 | tf_op jit(solution)/shard_map/ppermute | solution.py:380
  10.2 44.9 %collective-permute-start.6 = (bf16[16,256,256]{2,1,0:T(8,128)(2,1)}, bf16[16,256,256]{2,1,0:T(8,128)(2,1)}, u32[]{:S(2)}, u32[]{:S(2)}) collective-permute-start(bf16[16,256,256]{2,1,0:T(8,128)(2,1)} %bitcast.37), channel_id=1, source_target_pairs={{8,0},{12,4},{16,8},{20,12},{24,16},{28,20},{0,24},{4,28},{9,1},{1... | collective-permute-start | bytes 6291464 | tf_op jit(solution)/shard_map/ppermute | solution.py:380
  11.6 43.4 %collective-permute-start.5 = (bf16[16,256,256]{2,1,0:T(8,128)(2,1)}, bf16[16,256,256]{2,1,0:T(8,128)(2,1)}, u32[]{:S(2)}, u32[]{:S(2)}) collective-permute-start(bf16[16,256,256]{2,1,0:T(8,128)(2,1)} %bitcast.38), channel_id=1, source_target_pairs={{4,0},{12,8},{20,16},{28,24},{5,1},{13,9},{21,17},{29,25},{6,2},{1... | collective-permute-start | bytes 6291464 | tf_op jit(solution)/shard_map/ppermute | solution.py:380
  20.7 80.0 %collective-permute-start.3 = (bf16[16,256,256]{2,1,0:T(8,128)(2,1)}, bf16[16,256,256]{2,1,0:T(8,128)(2,1)}, u32[]{:S(2)}, u32[]{:S(2)}) collective-permute-start(bf16[16,256,256]{2,1,0:T(8,128)(2,1)} %collective-permute-done.1.refs_2_), channel_id=1, source_target_pairs={{2,3},{1,0},{6,7},{5,4},{10,11},{9,8},{14,15},{13,12},{18,19},{17,... | collective-permute-start | bytes 6291464 | tf_op jit(solution)/shard_map/ppermute | solution.py:350
  52.1 7.2 %copy-start.5 = (bf16[16,256,256]{2,1,0:T(8,128)(2,1)}, bf16[16,256,256]{2,1,0:T(8,128)(2,1)S(1)}, u32[]{:S(2)}) copy-start(bf16[16,256,256]{2,1,0:T(8,128)(2,1)S(1)} %collective-permute-done.refs_1_) | copy-start | bytes 6291460
  52.2 5.8 %collective-permute-start.10 = (bf16[8,256,256]{2,1,0:T(8,128)(2,1)S(1)}, bf16[8,256,256]{2,1,0:T(8,128)(2,1)}, u32[]{:S(2)}, u32[]{:S(2)}) collective-permute-start(bf16[8,256,256]{2,1,0:T(8,128)(2,1)S(1)} %slice.46), channel_id=1, source_target_pairs={{1,2},{2,1},{5,6},{6,5},{9,10},{10,9},{13,14},{14,13},{17,18},{18,... | collective-permute-start | bytes 3145736 | tf_op jit(solution)/shard_map/ppermute | solution.py:353
  55.1 4.3 %collective-permute-start.8 = (bf16[5,256,256]{2,1,0:T(8,128)(2,1)S(1)}, bf16[5,256,256]{2,1,0:T(8,128)(2,1)S(1)}, u32[]{:S(2)}, u32[]{:S(2)}) collective-permute-start(bf16[5,256,256]{2,1,0:T(8,128)(2,1)S(1)} %slice.45), channel_id=1, source_target_pairs={{1,2},{2,1},{5,6},{6,5},{9,10},{10,9},{13,14},{14,13},{17,18},{18,... | collective-permute-start | bytes 1966088 | tf_op jit(solution)/shard_map/ppermute | solution.py:353
  57.4 45.9 %collective-permute-start.13 = (bf16[8,256,256]{2,1,0:T(8,128)(2,1)S(1)}, bf16[8,256,256]{2,1,0:T(8,128)(2,1)S(1)}, u32[]{:S(2)}, u32[]{:S(2)}) collective-permute-start(bf16[8,256,256]{2,1,0:T(8,128)(2,1)S(1)} %get-tuple-element.48), channel_id=1, source_target_pairs={{0,4},{4,0},{8,12},{12,8},{16,20},{20,16},{24,28},{28,24},{1,5},{5... | collective-permute-start | bytes 3145736 | tf_op jit(solution)/shard_map/ppermute | solution.py:392
  57.5 45.8 %collective-permute-start.12 = (bf16[8,256,256]{2,1,0:T(8,128)(2,1)S(1)}, bf16[8,256,256]{2,1,0:T(8,128)(2,1)}, u32[]{:S(2)}, u32[]{:S(2)}) collective-permute-start(bf16[8,256,256]{2,1,0:T(8,128)(2,1)S(1)} %get-tuple-element.49), channel_id=1, source_target_pairs={{0,4},{4,0},{8,12},{12,8},{16,20},{20,16},{24,28},{28,24},{1,5},{5... | collective-permute-start | bytes 3145736 | tf_op jit(solution)/shard_map/ppermute | solution.py:392
  58.0 65.2 %collective-permute-start.11 = (bf16[8,256,256]{2,1,0:T(8,128)(2,1)}, bf16[8,256,256]{2,1,0:T(8,128)(2,1)}, u32[]{:S(2)}, u32[]{:S(2)}) collective-permute-start(bf16[8,256,256]{2,1,0:T(8,128)(2,1)} %collective-permute-done.10.refs_0_), channel_id=1, source_target_pairs={{2,3},{1,0},{6,7},{5,4},{10,11},{9,8},{14,15},{13,12},{18,19},{17,... | collective-permute-start | bytes 3145736 | tf_op jit(solution)/shard_map/ppermute | solution.py:357
  59.4 42.7 %collective-permute-start.2 = (bf16[3,256,256]{2,1,0:T(8,128)(2,1)S(1)}, bf16[3,256,256]{2,1,0:T(8,128)(2,1)S(1)}, u32[]{:S(2)}, u32[]{:S(2)}) collective-permute-start(bf16[3,256,256]{2,1,0:T(8,128)(2,1)S(1)} %slice.44), channel_id=1, source_target_pairs={{1,2},{2,1},{5,6},{6,5},{9,10},{10,9},{13,14},{14,13},{17,18},{18,... | collective-permute-start | bytes 1179656 | tf_op jit(solution)/shard_map/ppermute | solution.py:353
  100.7 36.4 %collective-permute-start.9 = (bf16[5,256,256]{2,1,0:T(8,128)(2,1)S(1)}, bf16[5,256,256]{2,1,0:T(8,128)(2,1)S(1)}, u32[]{:S(2)}, u32[]{:S(2)}) collective-permute-start(bf16[5,256,256]{2,1,0:T(8,128)(2,1)S(1)} %collective-permute-done.8.refs_0_), channel_id=1, source_target_pairs={{2,3},{1,0},{6,7},{5,4},{10,11},{9,8},{14,15},{13,12},{18,19},{17,... | collective-permute-start | bytes 1966088 | tf_op jit(solution)/shard_map/ppermute | solution.py:357
  102.0 41.7 %collective-permute-start.4 = (bf16[3,256,256]{2,1,0:T(8,128)(2,1)S(1)}, bf16[3,256,256]{2,1,0:T(8,128)(2,1)S(1)}, u32[]{:S(2)}, u32[]{:S(2)}) collective-permute-start(bf16[3,256,256]{2,1,0:T(8,128)(2,1)S(1)} %collective-permute-done.2.refs_0_), channel_id=1, source_target_pairs={{2,3},{1,0},{6,7},{5,4},{10,11},{9,8},{14,15},{13,12},{18,19},{17,... | collective-permute-start | bytes 1179656 | tf_op jit(solution)/shard_map/ppermute | solution.py:357
  103.3 1.0 copy-start.6
  123.2 13.9 %copy-start.2 = (bf16[10,256,256]{2,1,0:T(8,128)(2,1)S(1)}, bf16[10,256,256]{2,1,0:T(8,128)(2,1)}, u32[]{:S(2)}) copy-start(bf16[10,256,256]{2,1,0:T(8,128)(2,1)} %get-tuple-element.31.refs_3_) | copy-start | bytes 3932164
  123.2 13.9 %copy-start.4 = (s32[376]{0:T(512)S(1)}, s32[376]{0:T(512)}, u32[]{:S(2)}) copy-start(s32[376]{0:T(512)} %concatenate.37.table_ref) | copy-start | bytes 4516
  137.1 1.7 %copy-start = (f32[10,256,256]{2,1,0:T(8,128)S(1)}, f32[10,256,256]{2,1,0:T(8,128)}, u32[]{:S(2)}) copy-start(f32[10,256,256]{2,1,0:T(8,128)} %get-tuple-element.30.refs_2_) | copy-start | bytes 7864324
  138.9 1.4 copy-start.1
  140.3 3.5 %copy-start.3 = (bf16[6,256,256]{2,1,0:T(8,128)(2,1)S(1)}, bf16[6,256,256]{2,1,0:T(8,128)(2,1)}, u32[]{:S(2)}) copy-start(bf16[6,256,256]{2,1,0:T(8,128)(2,1)} %get-tuple-element.35.refs_3_) | copy-start | bytes 2359300

commit v4 on v3

--- a/solution.py
+++ b/solution.py
@@ -454,7 +454,7 @@
     own_rows, own_cols = c_rows[row_id, col_id], c_cols[row_id, col_id]
     on_line = lax.axis_size("col") == STEPS
     blocks = left.shape[0]
-    far_sizes = (blocks // 2, blocks - blocks // 2 - 3 * blocks // 16, 3 * blocks // 16)
+    far_sizes = (blocks - 2 * (blocks // 4), blocks // 4, blocks // 4 - blocks // 8, blocks // 8)
     columns = (line_columns if on_line else ring_columns)(col_id)
     picks, slots = pair_tables(columns, a_rows, a_inner, b_inner, b_cols, own_rows, own_cols)
     at_end = on_line & ((col_id == 0) | (col_id == 3))

time: 146 us -> 150 us (1.027)
  the two profiles are of different devices: /device:TPU:0 before, /device:TPU:10 now
where the time goes in v4:
time: 150 us; the launch traced here: 149 us
  waiting for transfers between devices  66.9 us (45%)
  starting transfers between devices  36 us (24%)
  Pallas kernels  32.5 us (22%)
  local copies, waits for them, and re-layouts  11.5 us (8%)
  other arithmetic  2.14 us (1%)
    ppermute x1, waiting for transfers between devices, line_of_four(): mid_in = lax.ppermute(left, 'col', cross)  32.8 us
    ppermute x3, waiting for transfers between devices, send(): return lax.ppermute(value, 'row', pairs)  17.7 us
    pallas_call x1, Pallas kernels, main_call(): pl.pallas_call(functools.partial(main_kernel, routes, takers, pieces, lay...  17 us
    ppermute x4, starting transfers between devices, line_of_four(): lax.ppermute(after(piece, *fetched) if place == 1 else piece, 'col', cross)  13.9 us
    ppermute x4, waiting for transfers between devices, line_of_four(): lax.ppermute(after(piece, *fetched) if place == 1 else piece, 'col', cross)  13.9 us
    pallas_call x3, Pallas kernels, piece_call(): pl.pallas_call(functools.partial(piece_kernel, len(lasts), later, fresh,...  13.6 us
    ppermute x4, starting transfers between devices, line_of_four(): lax.ppermute(after(piece, mid_out) if place else piece, 'col', out)  9.3 us
    ppermute x3, starting transfers between devices, send(): return lax.ppermute(value, 'row', pairs)  5.7 us
  transfers between devices with their start and end apart: 16, of which 5 were waited for; matrix products, arithmetic and copies ran while one was open for 7% of the time, Pallas kernels for 21%

profile of v4, /device:TPU:10, one launch (start us, length us, event | category | flops | bytes accessed | tf_op | source)
XLA Modules:
  0.0 149.5 jit_solution(6623606246597837843)
XLA Ops:
  0.0 3.5 %collective-permute-start.1 = (bf16[16,256,256]{2,1,0:T(8,128)(2,1)}, bf16[16,256,256]{2,1,0:T(8,128)(2,1)}, u32[]{:S(2)}, u32[]{:S(2)}) collective-permute-start(bf16[16,256,256]{2,1,0:T(8,128)(2,1)} %bitcast.33), channel_id=1, source_target_pairs={{1,2},{2,1},{5,6},{6,5},{9,10},{10,9},{13,14},{14,13},{17,18},{18,... | collective-permute-start | bytes 6291464 | tf_op jit(solution)/shard_map/ppermute | solution.py:349
  3.6 3.9 %collective-permute-start.9 = (bf16[16,256,256]{2,1,0:T(8,128)(2,1)}, bf16[16,256,256]{2,1,0:T(8,128)(2,1)}, u32[]{:S(2)}, u32[]{:S(2)}) collective-permute-start(bf16[16,256,256]{2,1,0:T(8,128)(2,1)} %bitcast.36), channel_id=1, source_target_pairs={{16,4},{24,12},{0,20},{8,28},{17,5},{25,13},{1,21},{9,29},{18,6},{... | collective-permute-start | bytes 6291464 | tf_op jit(solution)/shard_map/ppermute | solution.py:380
  7.5 0.5 collective-permute-start.8
  8.0 1.3 collective-permute-start.7
  9.4 0.7 dynamic-slice_bitcast_fusion
  10.1 0.6 gather_fusion.2
  10.7 0.6 gather_fusion
  11.2 0.7 constant_dynamic-slice_fusion.1
  12.0 0.6 gather_fusion.3
  12.6 0.6 gather_fusion.1
  13.1 0.3 fusion
  13.6 0.7 fusion.6
  14.4 0.3 select_reduce_fusion.1
  14.7 0.3 select_reduce_fusion
  15.1 0.1 copy.32
  15.5 0.1 copy.34
  15.9 0.2 select_reduce_fusion.3
  16.2 0.3 convert_reduce_fusion.2
  16.5 0.2 select_reduce_fusion.2
  16.8 32.8 %collective-permute-done.1.refs_2_ = bf16[16,256,256]{2,1,0:T(8,128)(2,1)} collective-permute-done((bf16[16,256,256]{2,1,0:T(8,128)(2,1)}, bf16[16,256,256]{2,1,0:T(8,128)(2,1)}, u32[]{:S(2)}, u32[]{:S(2)}) %collective-permute-start.1) | collective-permute-done | bytes 2097184 | tf_op jit(solution)/shard_map/ppermute | solution.py:349
  49.6 2.6 %collective-permute-start.3 = (bf16[16,256,256]{2,1,0:T(8,128)(2,1)}, bf16[16,256,256]{2,1,0:T(8,128)(2,1)}, u32[]{:S(2)}, u32[]{:S(2)}) collective-permute-start(bf16[16,256,256]{2,1,0:T(8,128)(2,1)} %collective-permute-done.1.refs_2_), channel_id=1, source_target_pairs={{2,3},{1,0},{6,7},{5,4},{10,11},{9,8},{14,15},{13,12},{18,19},{17,... | collective-permute-start | bytes 6291464 | tf_op jit(solution)/shard_map/ppermute | solution.py:350
  52.2 0.1 copy.30
  52.3 0.1 reshape.391
  52.5 0.1 copy.27
  52.6 0.1 add.123
  52.7 0.7 concatenate.41.table_ref
  53.5 3.5 %collective-permute-start.12 = (bf16[8,256,256]{2,1,0:T(8,128)(2,1)S(1)}, bf16[8,256,256]{2,1,0:T(8,128)(2,1)}, u32[]{:S(2)}, u32[]{:S(2)}) collective-permute-start(bf16[8,256,256]{2,1,0:T(8,128)(2,1)S(1)} %slice.59), channel_id=1, source_target_pairs={{1,2},{2,1},{5,6},{6,5},{9,10},{10,9},{13,14},{14,13},{17,18},{18,... | collective-permute-start | bytes 3145736 | tf_op jit(solution)/shard_map/ppermute | solution.py:353
  57.1 17.7 %collective-permute-done.9.refs_7_ = bf16[16,256,256]{2,1,0:T(8,128)(2,1)} collective-permute-done((bf16[16,256,256]{2,1,0:T(8,128)(2,1)}, bf16[16,256,256]{2,1,0:T(8,128)(2,1)}, u32[]{:S(2)}, u32[]{:S(2)}) %collective-permute-start.9) | collective-permute-done | bytes 2097184 | tf_op jit(solution)/shard_map/ppermute | solution.py:380
  74.7 3.5 %collective-permute-start.10 = (bf16[4,256,256]{2,1,0:T(8,128)(2,1)S(1)}, bf16[4,256,256]{2,1,0:T(8,128)(2,1)S(1)}, u32[]{:S(2)}, u32[]{:S(2)}) collective-permute-start(bf16[4,256,256]{2,1,0:T(8,128)(2,1)S(1)} %slice.58), channel_id=1, source_target_pairs={{1,2},{2,1},{5,6},{6,5},{9,10},{10,9},{13,14},{14,13},{17,18},{18,... | collective-permute-start | bytes 1572872 | tf_op jit(solution)/shard_map/ppermute | solution.py:353
  78.2 1.7 %fusion.16 = (bf16[8,256,256]{2,1,0:T(8,128)(2,1)S(1)}, bf16[8,256,256]{2,1,0:T(8,128)(2,1)S(1)}) fusion(bf16[16,256,256]{2,1,0:T(8,128)(2,1)} %collective-permute-done.8.refs_6_), kind=kLoop, calls=%fused_computation.80 | loop fusion | bytes 4194304 | tf_op jit(solution)/shard_map/slice | solution.py:392
  79.9 0.9 collective-permute-start.15
  80.8 2.3 %collective-permute-start.13 = (bf16[8,256,256]{2,1,0:T(8,128)(2,1)}, bf16[8,256,256]{2,1,0:T(8,128)(2,1)}, u32[]{:S(2)}, u32[]{:S(2)}) collective-permute-start(bf16[8,256,256]{2,1,0:T(8,128)(2,1)} %collective-permute-done.12.refs_0_), channel_id=1, source_target_pairs={{2,3},{1,0},{6,7},{5,4},{10,11},{9,8},{14,15},{13,12},{18,19},{17,... | collective-permute-start | bytes 3145736 | tf_op jit(solution)/shard_map/ppermute | solution.py:357
  83.2 8.1 %collective-permute-done.10.refs_0_ = bf16[4,256,256]{2,1,0:T(8,128)(2,1)S(1)} collective-permute-done((bf16[4,256,256]{2,1,0:T(8,128)(2,1)S(1)}, bf16[4,256,256]{2,1,0:T(8,128)(2,1)S(1)}, u32[]{:S(2)}, u32[]{:S(2)}) %collective-permute-start.10) | collective-permute-done | bytes 524320 | tf_op jit(solution)/shard_map/ppermute | solution.py:353
  91.3 3.5 %collective-permute-start.5 = (bf16[2,256,256]{2,1,0:T(8,128)(2,1)S(1)}, bf16[2,256,256]{2,1,0:T(8,128)(2,1)S(1)}, u32[]{:S(2)}, u32[]{:S(2)}) collective-permute-start(bf16[2,256,256]{2,1,0:T(8,128)(2,1)S(1)} %get-tuple-element.68), channel_id=1, source_target_pairs={{1,2},{2,1},{5,6},{6,5},{9,10},{10,9},{13,14},{14,13},{17,18},{18,... | collective-permute-start | bytes 786440 | tf_op jit(solution)/shard_map/ppermute | solution.py:353
  94.8 2.5 %collective-permute-done.3.refs_3_ = bf16[16,256,256]{2,1,0:T(8,128)(2,1)} collective-permute-done((bf16[16,256,256]{2,1,0:T(8,128)(2,1)}, bf16[16,256,256]{2,1,0:T(8,128)(2,1)}, u32[]{:S(2)}, u32[]{:S(2)}) %collective-permute-start.3) | collective-permute-done | bytes 2097184 | tf_op jit(solution)/shard_map/ppermute | solution.py:350
  97.2 4.4 %collective-permute-start.11 = (bf16[4,256,256]{2,1,0:T(8,128)(2,1)S(1)}, bf16[4,256,256]{2,1,0:T(8,128)(2,1)S(1)}, u32[]{:S(2)}, u32[]{:S(2)}) collective-permute-start(bf16[4,256,256]{2,1,0:T(8,128)(2,1)S(1)} %collective-permute-done.10.refs_0_), channel_id=1, source_target_pairs={{2,3},{1,0},{6,7},{5,4},{10,11},{9,8},{14,15},{13,12},{18,19},{17,... | collective-permute-start | bytes 1572872 | tf_op jit(solution)/shard_map/ppermute | solution.py:357
  101.7 3.5 %collective-permute-start.2 = (bf16[2,256,256]{2,1,0:T(8,128)(2,1)S(1)}, bf16[2,256,256]{2,1,0:T(8,128)(2,1)S(1)}, u32[]{:S(2)}, u32[]{:S(2)}) collective-permute-start(bf16[2,256,256]{2,1,0:T(8,128)(2,1)S(1)} %get-tuple-element.69), channel_id=1, source_target_pairs={{1,2},{2,1},{5,6},{6,5},{9,10},{10,9},{13,14},{14,13},{17,18},{18,... | collective-permute-start | bytes 786440 | tf_op jit(solution)/shard_map/ppermute | solution.py:353
  105.2 5.7 %collective-permute-done.2.refs_0_ = bf16[2,256,256]{2,1,0:T(8,128)(2,1)S(1)} collective-permute-done((bf16[2,256,256]{2,1,0:T(8,128)(2,1)S(1)}, bf16[2,256,256]{2,1,0:T(8,128)(2,1)S(1)}, u32[]{:S(2)}, u32[]{:S(2)}) %collective-permute-start.2) | collective-permute-done | bytes 262176 | tf_op jit(solution)/shard_map/ppermute | solution.py:353
  110.9 1.3 collective-permute-start.6
  112.2 1.3 collective-permute-start.4
  113.5 17.0 %first_panels.1 = (bf16[64,256,256]{2,1,0:T(8,128)(2,1)}, f32[16,256,256]{2,1,0:T(8,128)}, f32[8,256,256]{2,1,0:T(8,128)}, f32[4,256,256]{2,1,0:T(8,128)}, f32[4...) custom-call(s32[382]{0:T(512)} %concatenate.41.table_ref, ...), custom_call_target="tpu_custom_call" | custom-call | flops 1048576 | bytes 65536 | tf_op jit(solution)/shard_map/first_panels/pallas_call | solution.py:145
  130.6 6.9 %last_panel_piece.3 = (bf16[64,256,256]{2,1,0:T(8,128)(2,1)}, f32[8,256,256]{2,1,0:T(8,128)}, f32[4,256,256]{2,1,0:T(8,128)}, f32[4,256,256]{2,1,0:T(8,128)}) custom-call(s32[382]{0:T(512)} %concatenate.41.table_ref, bf16[8,256,256]{2,1,0:T(8,128)(2,1)} %collective-permute-done.12.refs_0_, ...), custom_call_target="tpu_custom_call", output_to_operand_aliasing={{0}: (5, {}), {1}: (6, {}), {2}: (7, {}), {3}: (8, {})} | custom-call | flops 1048576 | bytes 65536 | tf_op jit(solution)/shard_map/last_panel_piece/pallas_call | solution.py:243
  137.5 0.8 copy-done.7
  138.3 4.8 %last_panel_piece.4 = (bf16[64,256,256]{2,1,0:T(8,128)(2,1)}, f32[4,256,256]{2,1,0:T(8,128)}, f32[4,256,256]{2,1,0:T(8,128)}) custom-call(s32[382]{0:T(512)} %concatenate.41.table_ref, bf16[4,256,256]{2,1,0:T(8,128)(2,1)} %copy-done.6, bf16[4,256,256]{2,1,0:T(8,128)(2,1)} %copy-done.7, ...), custom_call_target="tpu_custom_call", output_to_operand_aliasing={{0}: (5, {}), {1}: (6, {}), {2}: (7, {})} | custom-call | flops 1048576 | bytes 65536 | tf_op jit(solution)/shard_map/last_panel_piece/pallas_call | solution.py:243
  143.1 1.2 copy-done
  144.3 1.2 copy-done.1
  145.5 2.0 %last_panel_piece.5 = (bf16[64,256,256]{2,1,0:T(8,128)(2,1)}, f32[4,256,256]{2,1,0:T(8,128)S(1)}) custom-call(s32[382]{0:T(512)S(1)} %copy-done.4, bf16[2,256,256]{2,1,0:T(8,128)(2,1)S(1)} %collective-permute-done.5.refs_0_, bf16[2,256,256]{2,1,0:T(8,128)(2,1)S(1)} %collective-permute-done.6.refs_1_, ...), custom_call_target="tpu_custom_call", output_to_operand_aliasing={{0}: (5, {})} | custom-call | flops 1048576 | bytes 65536 | tf_op jit(solution)/shard_map/last_panel_piece/pallas_call | solution.py:243
  147.6 1.9 %last_piece.1 = bf16[64,256,256]{2,1,0:T(8,128)(2,1)} custom-call(s32[382]{0:T(512)S(1)} %copy-done.4, bf16[2,256,256]{2,1,0:T(8,128)(2,1)S(1)} %collective-permute-done.2.refs_0_, bf16[2,256,256]{2,1,0:T(8,128)(2,1)S(1)} %collective-permute-done.4.refs_1_, f32[4,256,256]{2,1,0:T(8,128)S(1)} %get-tuple-element.48.refs_2_, ...), custom_call_target="tpu_custom_call", output_to_operand_aliasing={{}: (5, {})} | custom-call | flops 1048576 | bytes 65536 | tf_op jit(solution)/shard_map/last_piece/pallas_call | solution.py:308
  (59 shorter events, 1.6 us)
Async XLA Ops:
  0.0 49.6 %collective-permute-start.1 = (bf16[16,256,256]{2,1,0:T(8,128)(2,1)}, bf16[16,256,256]{2,1,0:T(8,128)(2,1)}, u32[]{:S(2)}, u32[]{:S(2)}) collective-permute-start(bf16[16,256,256]{2,1,0:T(8,128)(2,1)} %bitcast.33), channel_id=1, source_target_pairs={{1,2},{2,1},{5,6},{6,5},{9,10},{10,9},{13,14},{14,13},{17,18},{18,... | collective-permute-start | bytes 6291464 | tf_op jit(solution)/shard_map/ppermute | solution.py:349
  3.5 50.0 %collective-permute-start = (bf16[16,256,256]{2,1,0:T(8,128)(2,1)}, bf16[16,256,256]{2,1,0:T(8,128)(2,1)S(1)}, u32[]{:S(2)}, u32[]{:S(2)}) collective-permute-start(bf16[16,256,256]{2,1,0:T(8,128)(2,1)} %bitcast.34), channel_id=1, source_target_pairs={{0,1},{1,0},{2,3},{3,2},{4,5},{5,4},{6,7},{7,6},{8,9},{9,8},{10,11... | collective-permute-start | bytes 6291464 | tf_op jit(solution)/shard_map/ppermute | solution.py:348
  3.6 71.2 %collective-permute-start.9 = (bf16[16,256,256]{2,1,0:T(8,128)(2,1)}, bf16[16,256,256]{2,1,0:T(8,128)(2,1)}, u32[]{:S(2)}, u32[]{:S(2)}) collective-permute-start(bf16[16,256,256]{2,1,0:T(8,128)(2,1)} %bitcast.36), channel_id=1, source_target_pairs={{16,4},{24,12},{0,20},{8,28},{17,5},{25,13},{1,21},{9,29},{18,6},{... | collective-permute-start | bytes 6291464 | tf_op jit(solution)/shard_map/ppermute | solution.py:380
  7.5 67.3 %collective-permute-start.8 = (bf16[16,256,256]{2,1,0:T(8,128)(2,1)}, bf16[16,256,256]{2,1,0:T(8,128)(2,1)}, u32[]{:S(2)}, u32[]{:S(2)}) collective-permute-start(bf16[16,256,256]{2,1,0:T(8,128)(2,1)} %bitcast.37), channel_id=1, source_target_pairs={{8,0},{12,4},{16,8},{20,12},{24,16},{28,20},{0,24},{4,28},{9,1},{1... | collective-permute-start | bytes 6291464 | tf_op jit(solution)/shard_map/ppermute | solution.py:380
  8.0 66.7 %collective-permute-start.7 = (bf16[16,256,256]{2,1,0:T(8,128)(2,1)}, bf16[16,256,256]{2,1,0:T(8,128)(2,1)}, u32[]{:S(2)}, u32[]{:S(2)}) collective-permute-start(bf16[16,256,256]{2,1,0:T(8,128)(2,1)} %bitcast.38), channel_id=1, source_target_pairs={{4,0},{12,8},{20,16},{28,24},{5,1},{13,9},{21,17},{29,25},{6,2},{1... | collective-permute-start | bytes 6291464 | tf_op jit(solution)/shard_map/ppermute | solution.py:380
  49.6 47.7 %collective-permute-start.3 = (bf16[16,256,256]{2,1,0:T(8,128)(2,1)}, bf16[16,256,256]{2,1,0:T(8,128)(2,1)}, u32[]{:S(2)}, u32[]{:S(2)}) collective-permute-start(bf16[16,256,256]{2,1,0:T(8,128)(2,1)} %collective-permute-done.1.refs_2_), channel_id=1, source_target_pairs={{2,3},{1,0},{6,7},{5,4},{10,11},{9,8},{14,15},{13,12},{18,19},{17,... | collective-permute-start | bytes 6291464 | tf_op jit(solution)/shard_map/ppermute | solution.py:350
  53.4 29.7 %copy-start.5 = (bf16[16,256,256]{2,1,0:T(8,128)(2,1)}, bf16[16,256,256]{2,1,0:T(8,128)(2,1)S(1)}, u32[]{:S(2)}) copy-start(bf16[16,256,256]{2,1,0:T(8,128)(2,1)S(1)} %collective-permute-done.refs_1_) | copy-start | bytes 6291460
  53.5 27.3 %collective-permute-start.12 = (bf16[8,256,256]{2,1,0:T(8,128)(2,1)S(1)}, bf16[8,256,256]{2,1,0:T(8,128)(2,1)}, u32[]{:S(2)}, u32[]{:S(2)}) collective-permute-start(bf16[8,256,256]{2,1,0:T(8,128)(2,1)S(1)} %slice.59), channel_id=1, source_target_pairs={{1,2},{2,1},{5,6},{6,5},{9,10},{10,9},{13,14},{14,13},{17,18},{18,... | collective-permute-start | bytes 3145736 | tf_op jit(solution)/shard_map/ppermute | solution.py:353
  74.7 16.6 %collective-permute-start.10 = (bf16[4,256,256]{2,1,0:T(8,128)(2,1)S(1)}, bf16[4,256,256]{2,1,0:T(8,128)(2,1)S(1)}, u32[]{:S(2)}, u32[]{:S(2)}) collective-permute-start(bf16[4,256,256]{2,1,0:T(8,128)(2,1)S(1)} %slice.58), channel_id=1, source_target_pairs={{1,2},{2,1},{5,6},{6,5},{9,10},{10,9},{13,14},{14,13},{17,18},{18,... | collective-permute-start | bytes 1572872 | tf_op jit(solution)/shard_map/ppermute | solution.py:353
  79.9 32.3 %collective-permute-start.15 = (bf16[8,256,256]{2,1,0:T(8,128)(2,1)S(1)}, bf16[8,256,256]{2,1,0:T(8,128)(2,1)}, u32[]{:S(2)}, u32[]{:S(2)}) collective-permute-start(bf16[8,256,256]{2,1,0:T(8,128)(2,1)S(1)} %get-tuple-element.66), channel_id=1, source_target_pairs={{0,4},{4,0},{8,12},{12,8},{16,20},{20,16},{24,28},{28,24},{1,5},{5... | collective-permute-start | bytes 3145736 | tf_op jit(solution)/shard_map/ppermute | solution.py:392
  80.8 32.8 %collective-permute-start.14 = (bf16[8,256,256]{2,1,0:T(8,128)(2,1)S(1)}, bf16[8,256,256]{2,1,0:T(8,128)(2,1)}, u32[]{:S(2)}, u32[]{:S(2)}) collective-permute-start(bf16[8,256,256]{2,1,0:T(8,128)(2,1)S(1)} %get-tuple-element.67), channel_id=1, source_target_pairs={{0,4},{4,0},{8,12},{12,8},{16,20},{20,16},{24,28},{28,24},{1,5},{5... | collective-permute-start | bytes 3145736 | tf_op jit(solution)/shard_map/ppermute | solution.py:392
  80.8 49.7 %collective-permute-start.13 = (bf16[8,256,256]{2,1,0:T(8,128)(2,1)}, bf16[8,256,256]{2,1,0:T(8,128)(2,1)}, u32[]{:S(2)}, u32[]{:S(2)}) collective-permute-start(bf16[8,256,256]{2,1,0:T(8,128)(2,1)} %collective-permute-done.12.refs_0_), channel_id=1, source_target_pairs={{2,3},{1,0},{6,7},{5,4},{10,11},{9,8},{14,15},{13,12},{18,19},{17,... | collective-permute-start | bytes 3145736 | tf_op jit(solution)/shard_map/ppermute | solution.py:357
  91.3 39.3 %copy-start.6 = (bf16[4,256,256]{2,1,0:T(8,128)(2,1)}, bf16[4,256,256]{2,1,0:T(8,128)(2,1)S(1)}, u32[]{:S(2)}) copy-start(bf16[4,256,256]{2,1,0:T(8,128)(2,1)S(1)} %collective-permute-done.10.refs_0_) | copy-start | bytes 1572868
  91.3 10.3 %collective-permute-start.5 = (bf16[2,256,256]{2,1,0:T(8,128)(2,1)S(1)}, bf16[2,256,256]{2,1,0:T(8,128)(2,1)S(1)}, u32[]{:S(2)}, u32[]{:S(2)}) collective-permute-start(bf16[2,256,256]{2,1,0:T(8,128)(2,1)S(1)} %get-tuple-element.68), channel_id=1, source_target_pairs={{1,2},{2,1},{5,6},{6,5},{9,10},{10,9},{13,14},{14,13},{17,18},{18,... | collective-permute-start | bytes 786440 | tf_op jit(solution)/shard_map/ppermute | solution.py:353
  97.2 40.2 %collective-permute-start.11 = (bf16[4,256,256]{2,1,0:T(8,128)(2,1)S(1)}, bf16[4,256,256]{2,1,0:T(8,128)(2,1)S(1)}, u32[]{:S(2)}, u32[]{:S(2)}) collective-permute-start(bf16[4,256,256]{2,1,0:T(8,128)(2,1)S(1)} %collective-permute-done.10.refs_0_), channel_id=1, source_target_pairs={{2,3},{1,0},{6,7},{5,4},{10,11},{9,8},{14,15},{13,12},{18,19},{17,... | collective-permute-start | bytes 1572872 | tf_op jit(solution)/shard_map/ppermute | solution.py:357
  101.7 9.2 %collective-permute-start.2 = (bf16[2,256,256]{2,1,0:T(8,128)(2,1)S(1)}, bf16[2,256,256]{2,1,0:T(8,128)(2,1)S(1)}, u32[]{:S(2)}, u32[]{:S(2)}) collective-permute-start(bf16[2,256,256]{2,1,0:T(8,128)(2,1)S(1)} %get-tuple-element.69), channel_id=1, source_target_pairs={{1,2},{2,1},{5,6},{6,5},{9,10},{10,9},{13,14},{14,13},{17,18},{18,... | collective-permute-start | bytes 786440 | tf_op jit(solution)/shard_map/ppermute | solution.py:353
  110.9 32.2 %collective-permute-start.6 = (bf16[2,256,256]{2,1,0:T(8,128)(2,1)S(1)}, bf16[2,256,256]{2,1,0:T(8,128)(2,1)S(1)}, u32[]{:S(2)}, u32[]{:S(2)}) collective-permute-start(bf16[2,256,256]{2,1,0:T(8,128)(2,1)S(1)} %collective-permute-done.5.refs_0_), channel_id=1, source_target_pairs={{2,3},{1,0},{6,7},{5,4},{10,11},{9,8},{14,15},{13,12},{18,19},{17,... | collective-permute-start | bytes 786440 | tf_op jit(solution)/shard_map/ppermute | solution.py:357
  112.2 35.3 %collective-permute-start.4 = (bf16[2,256,256]{2,1,0:T(8,128)(2,1)S(1)}, bf16[2,256,256]{2,1,0:T(8,128)(2,1)S(1)}, u32[]{:S(2)}, u32[]{:S(2)}) collective-permute-start(bf16[2,256,256]{2,1,0:T(8,128)(2,1)S(1)} %collective-permute-done.2.refs_0_), channel_id=1, source_target_pairs={{2,3},{1,0},{6,7},{5,4},{10,11},{9,8},{14,15},{13,12},{18,19},{17,... | collective-permute-start | bytes 786440 | tf_op jit(solution)/shard_map/ppermute | solution.py:357
  137.5 0.8 copy-start.7
  138.3 4.8 %copy-start.3 = (bf16[4,256,256]{2,1,0:T(8,128)(2,1)S(1)}, bf16[4,256,256]{2,1,0:T(8,128)(2,1)}, u32[]{:S(2)}) copy-start(bf16[4,256,256]{2,1,0:T(8,128)(2,1)} %get-tuple-element.45.refs_3_) | copy-start | bytes 1572868
  138.3 4.8 %copy-start.4 = (s32[382]{0:T(512)S(1)}, s32[382]{0:T(512)}, u32[]{:S(2)}) copy-start(s32[382]{0:T(512)} %concatenate.41.table_ref) | copy-start | bytes 4588
  143.1 1.2 copy-start
  144.3 1.2 copy-start.1
  145.5 2.0 %copy-start.2 = (bf16[4,256,256]{2,1,0:T(8,128)(2,1)S(1)}, bf16[4,256,256]{2,1,0:T(8,128)(2,1)}, u32[]{:S(2)}) copy-start(bf16[4,256,256]{2,1,0:T(8,128)(2,1)} %get-tuple-element.49.refs_3_) | copy-start | bytes 1572868
